TPU v7x, 256 devices: a whole 4x4x8 slice. The times are simulated.
256 devices in a mesh: outer: 4 (over x), member: 64 (over y, z, core).
Axes of the slice: x: 4, y: 4, z: 8, core: 2. Of those that a mesh axis runs over, the one named last changes fastest.
Arguments:
- embeds: bfloat16 [524288, 768], P(('outer', 'member')), parts along dimension 0, as said below
- cluster_id: int32 [524288], P(('outer', 'member')), parts along dimension 0, may hold values from 0 to 255, as said below
- row_index: int32 [524288], P(('outer', 'member')), parts along dimension 0, may hold values from 0 to 131071, each once
Outputs:
- nearest: float32 [524288], P(('outer', 'member')), parts along dimension 0
There are 4 independent parts, one for each index of `outer`. A program takes and returns all parts, laid end to end along the dimension named above; each array names one. Nothing has to cross between parts.
Inputs may be any that keep to these rules, and one draw needn't show every extreme that they name: `cluster_id`: no cluster has more than 16 rows on one device; one cluster has exactly 16 rows on every device; the clusters of each owner hold exactly 256 / (devices of member) * 8 rows of every device. `embeds`: Real-valued rows with no zero row.
All inputs are finite; a program needn't handle non-finite values.
Results may differ from a plain program's by a relative error of at most 0.00063.
Values may be sent and summed in bfloat16 or wider, within the bound.
No kernel may reach another device: no remote copies, remote signals or barrier semaphores. Data moves between devices by JAX's collectives and lax.ppermute only.
A program may use at most 64 MiB of HBM per device.

v0:
```python
import jax
import jax.numpy as jnp
from jax import lax
from jax.sharding import PartitionSpec as P

CLUSTERS = 256


def earlier_best(pieces):
    blocks, orders = pieces
    senders, items, most, width = blocks.shape

    def one(inputs):
        block, order = inputs
        flat_rows = block.reshape(senders * most, width)
        flat_order = order.reshape(senders * most)
        scores = jnp.dot(flat_rows, flat_rows.T, preferred_element_type=jnp.float32)
        keep = (flat_order[None, :] < flat_order[:, None]) & (flat_order[None, :] >= 0)
        best = jnp.maximum(jnp.max(jnp.where(keep, scores, -1.0), axis=1), -1.0)
        return best.reshape(senders, most)

    result = lax.map(one, (jnp.swapaxes(blocks, 0, 1), jnp.swapaxes(orders, 0, 1)))
    return jnp.swapaxes(result, 0, 1)


def on_device(embeds, cluster_id, row_index):
    members = lax.axis_size("member")
    rows, width = embeds.shape
    clusters = CLUSTERS
    most = 2 * rows // clusters
    per_owner = clusters // members
    whole = embeds.astype(jnp.float32)
    inverse = lax.rsqrt(jnp.sum(whole * whole, axis=1, keepdims=True) + 1e-06)
    unit = (whole * inverse).astype(jnp.bfloat16)
    labels = jnp.arange(clusters, dtype=jnp.int32)
    match = (cluster_id[:, None] == labels[None, :]).astype(jnp.int32)
    rank = jnp.sum((jnp.cumsum(match, axis=0) - 1) * match, axis=1)
    target = cluster_id * most + rank
    outgoing = jnp.zeros((clusters * most, width), jnp.bfloat16).at[target].set(unit)
    out_order = jnp.full((clusters * most,), -1, jnp.int32).at[target].set(row_index)
    outgoing = outgoing.reshape(members, per_owner, most, width)
    out_order = out_order.reshape(members, per_owner, most)
    owned = earlier_best(
        (
            lax.all_to_all(outgoing, "member", split_axis=0, concat_axis=0, tiled=True),
            lax.all_to_all(out_order, "member", split_axis=0, concat_axis=0, tiled=True),
        )
    )
    returned = lax.all_to_all(owned, "member", split_axis=0, concat_axis=0, tiled=True)
    return returned.reshape(clusters * most)[target]


def solution(mesh):
    in_specs = (P(("outer", "member"), None), P(("outer", "member")), P(("outer", "member")))
    out_specs = P(("outer", "member"))
    return jax.shard_map(
        on_device, mesh=mesh, in_specs=in_specs, out_specs=out_specs, check_vma=False
    )
```

profile of v0, /device:TPU:1, one launch (start us, length us, event | category | flops | bytes accessed | tf_op | source)
XLA Modules:
  0.0 245.6 jit_solution(11081229308114097963)
XLA Ops:
  0.0 0.8 copy.9
  0.8 0.3 fusion.7
  1.2 0.3 add_add_fusion
  1.5 1.2 copy.10
  2.7 0.9 fusion.6
  3.6 8.2 %scatter_custom_fusion = s32[4096]{0:T(1024)S(1)} fusion(s32[2048]{0:T(1024)S(1)} %get-tuple-element.45, s32[2048]{0:T(1024)} %param.7, s32[]{:T(128)} %constant.21.clone.1), kind=kCustom, calls=%fused_computation.26 | custom fusion | bytes 16896 | tf_op jit(solution)/shard_map/scatter | solution.py:40
  11.9 0.8 reshape.66
  12.6 13.2 %all-to-all-start = ((s32[64,4,16]{2,1,0:T(4,128)}), s32[64,4,16]{2,1,0:T(4,128)S(1)}, u32[]{:S(2)}, u32[]{:S(2)}) async-start(s32[64,4,16]{2,1,0:T(4,128)} %reshape.66), calls=%async_computation | async-start | bytes 262144 | tf_op jit(solution)/shard_map/all_to_all | solution.py:46
  25.8 0.7 fusion
  26.5 14.2 %scatter_custom_fusion.1 = bf16[4096,768]{1,0:T(8,128)(2,1)} fusion(s32[2048]{0:T(1024)S(1)} %get-tuple-element.45, bf16[2048,768]{1,0:T(8,128)(2,1)S(1)} %copy-done, f32[2048]{0:T(1024)S(1)} %add_rsqrt_fusion, bf16[]{:T(256)} %constant.19.clone.1), kind=kCustom, calls=%fused_computation.12 | custom fusion | flops 4718592 | bytes 9445378 | tf_op jit(solution)/shard_map/scatter | solution.py:39
  40.7 10.5 %all-to-all-start.1 = ((bf16[64,4,16,768]{3,2,1,0:T(8,128)(2,1)}), bf16[64,4,16,768]{3,2,1,0:T(8,128)(2,1)}, u32[]{:S(2)}, u32[]{:S(2)}) async-start(bf16[64,4,16,768]{3,2,1,0:T(8,128)(2,1)} %bitcast.31), calls=%async_computation.1 | async-start | bytes 12582912 | tf_op jit(solution)/shard_map/all_to_all | solution.py:45
  51.3 140.8 %all-to-all-done.1 = bf16[64,4,16,768]{3,2,1,0:T(8,128)(2,1)} async-done(((bf16[64,4,16,768]{3,2,1,0:T(8,128)(2,1)}), bf16[64,4,16,768]{3,2,1,0:T(8,128)(2,1)}, u32[]{:S(2)}, u32[]{:S(2)}) %all-to-all-start.1) | async-done | bytes 6291488 | tf_op jit(solution)/shard_map/all_to_all | solution.py:45
  192.1 16.9 %while.10 = (s32[]{:T(128)}, f32[4,64,16]{2,0,1:T(4,128)S(1)}, s32[4,64,16]{2,0,1:T(4,128)S(1)}, bf16[4,64,16,768]{3,2,0,1:T(8,128)(2,1)}, s32[]{:T(128)}, /*index=5*/s32[]{:T(128)}) while((s32[]{:T(128)}, f32[4,64,16]{2,0,1:T(4,128)S(1)}, s32[4,64,16]{2,0,1:T(4,128)S(1)}, bf16[4,64,16,768]{3,2,0,1:T(8,128)(2,1)}, s32[]{:T(128)}, ...), condition=%wide.region_8.9_spmd, body=%wide.region_6.8_spmd.sunk | while | flops 1614808064 | bytes 4773969 | solution.py:22
  192.2 1.5 constant_dynamic-slice_fusion.5
  193.7 2.3 select_reduce_fusion.2
  196.1 0.2 dynamic_update_slice.5
  196.4 1.5 constant_dynamic-slice_fusion.5
  198.0 2.3 select_reduce_fusion.2
  200.7 1.5 constant_dynamic-slice_fusion.5
  202.2 2.3 select_reduce_fusion.2
  204.9 1.5 constant_dynamic-slice_fusion.5
  206.4 2.3 select_reduce_fusion.2
  209.0 15.9 %all_to_all.15 = f32[64,4,16]{2,1,0:T(4,128)S(1)} all-to-all(f32[64,4,16]{2,1,0:T(4,128)S(1)} %bitcast.35), channel_id=1, replica_groups=mesh['outer'=4,'member'=64] {'member'}, dimensions={0} | all-to-all | bytes 32768 | tf_op jit(solution)/shard_map/all_to_all | solution.py:49
  225.0 20.5 %gather_fusion = f32[2048]{0:T(1024)} fusion(f32[4096]{0:T(1024)S(1)} %reshape.68, s32[2048]{0:T(1024)S(1)} %get-tuple-element.44), kind=kCustom, calls=%fused_computation | custom fusion | bytes 24576 | tf_op jit(solution)/shard_map/gather | solution.py:50
  (35 shorter events, 1.5 us)
Async XLA Ops:
  1.5 1.3 copy-start.1
  1.5 24.3 %copy-start = (bf16[2048,768]{1,0:T(8,128)(2,1)S(1)}, bf16[2048,768]{1,0:T(8,128)(2,1)}, u32[]{:S(2)}) copy-start(bf16[2048,768]{1,0:T(8,128)(2,1)} %param.5) | copy-start | bytes 9437188
  12.6 28.1 %all-to-all-start = ((s32[64,4,16]{2,1,0:T(4,128)}), s32[64,4,16]{2,1,0:T(4,128)S(1)}, u32[]{:S(2)}, u32[]{:S(2)}) async-start(s32[64,4,16]{2,1,0:T(4,128)} %reshape.66), calls=%async_computation | async-start | bytes 262144 | tf_op jit(solution)/shard_map/all_to_all | solution.py:46
  40.7 151.3 %all-to-all-start.1 = ((bf16[64,4,16,768]{3,2,1,0:T(8,128)(2,1)}), bf16[64,4,16,768]{3,2,1,0:T(8,128)(2,1)}, u32[]{:S(2)}, u32[]{:S(2)}) async-start(bf16[64,4,16,768]{3,2,1,0:T(8,128)(2,1)} %bitcast.31), calls=%async_computation.1 | async-start | bytes 12582912 | tf_op jit(solution)/shard_map/all_to_all | solution.py:45
where the time goes:
time: 246 us
  waiting for transfers between devices  141 us (57%)
  local copies, waits for them, and re-layouts  39.2 us (16%)
  starting transfers between devices  23.7 us (10%)
  other arithmetic  16.5 us (7%)
  blocking collectives  15.9 us (6%)
  matrix products  9.12 us (4%)
    all_to_all x1, waiting for transfers between devices, on_device(): lax.all_to_all(outgoing, 'member', split_axis=0, concat_axis=0, tiled=True)  141 us
    gather x1, local copies, waits for them, and re-layouts, on_device(): return returned.reshape(clusters * most)[target]  20.5 us
    all_to_all x1, blocking collectives, on_device(): lax.all_to_all(owned, 'member', split_axis=0, concat_axis=0, tiled=True)  15.9 us
    scatter x1, other arithmetic, on_device(): jnp.zeros((clusters * most, width), jnp.bfloat16).at[target].set(unit)  14.2 us
    all_to_all x1, starting transfers between devices, on_device(): lax.all_to_all(out_order, 'member', split_axis=0, concat_axis=0, tiled=True)  13.2 us
    all_to_all x1, starting transfers between devices, on_device(): lax.all_to_all(outgoing, 'member', split_axis=0, concat_axis=0, tiled=True)  10.5 us
    dot_general x4, matrix products, one(): scores = jnp.dot(flat_rows, flat_rows.T, preferred_element_type=jnp.float32)  9.12 us
    scatter x1, local copies, waits for them, and re-layouts, on_device(): jnp.full((clusters * most,), -1, jnp.int32).at[target].set(row_index)  8.23 us
  transfers between devices with their start and end apart: 2, of which 1 were waited for; matrix products, arithmetic and copies ran while one was open for 6% of the time, Pallas kernels for 0%

commit v1 on v0

v1 whole, which is shorter than its diff:
```python
import functools

import jax
import jax.numpy as jnp
from jax import lax
from jax.experimental import pallas as pl
from jax.experimental.pallas import tpu as pltpu
from jax.sharding import PartitionSpec as P

CLUSTERS = 256
INDEX_BITS = 17
LANES = 128
META = 8


def iota(shape, dim):
    return lax.broadcasted_iota(jnp.int32, shape, dim)


def wide_row(ref):
    return jnp.concatenate([ref[b : b + 1, :] for b in range(ref.shape[0])], axis=1)


def send_kernel(owners, per_owner, per_pair, cid_ref, idx_ref, emb_ref, out_ref, pos_ref, pos_scr, meta_scr):
    rows, width = emb_ref.shape
    step = pl.program_id(0)
    per_step = out_ref.shape[0]
    size = per_step * per_pair

    @pl.when(step == 0)
    def _():
        cid = wide_row(cid_ref)
        idx = wide_row(idx_ref)
        owner = cid // per_owner
        hit = iota((owners, rows), 0) == owner
        hot = hit.astype(jnp.bfloat16)
        tile = 256
        before = (iota((tile, tile), 0) < iota((tile, tile), 1)).astype(jnp.bfloat16)
        carry = jnp.zeros((owners, 1), jnp.float32)
        ranks = []
        for b in range(rows // tile):
            part = hot[:, b * tile : (b + 1) * tile]
            wide = part.astype(jnp.float32)
            count = jnp.dot(part, before, preferred_element_type=jnp.float32) + carry
            ranks.append(jnp.sum(count * wide, axis=0, keepdims=True))
            carry = carry + jnp.sum(wide, axis=1, keepdims=True)
        rank = jnp.concatenate(ranks, axis=1).astype(jnp.int32)
        pos = owner * per_pair + rank
        pos_scr[...] = pos
        for b in range(pos_ref.shape[0]):
            pos_ref[b : b + 1, :] = pos[:, b * LANES : (b + 1) * LANES]
        key = (cid - owner * per_owner) * (1 << INDEX_BITS) + idx
        slot = iota((per_pair, rows), 0) == rank
        pieces = (key & 255, (key >> 8) & 255, key >> 16)
        spread = [jnp.where(slot, p.astype(jnp.float32), 0.0).astype(jnp.bfloat16) for p in pieces]
        spread.append(jnp.zeros((LANES - 3 * per_pair, rows), jnp.bfloat16))
        spread = jnp.concatenate(spread, axis=0)
        meta_scr[...] = lax.dot_general(
            hot, spread, (((1,), (1,)), ((), ())), preferred_element_type=jnp.float32
        )

    pick = (iota((size, rows), 0) + step * size == pos_scr[...]).astype(jnp.bfloat16)
    moved = jnp.dot(pick, emb_ref[...], preferred_element_type=jnp.float32)
    inverse = lax.rsqrt(jnp.sum(moved * moved, axis=1, keepdims=True) + 1e-06)
    unit = (moved * inverse).astype(jnp.bfloat16)
    for c in range(width // LANES):
        out_ref[:, c * per_pair : (c + 1) * per_pair, :] = unit[:, c * LANES : (c + 1) * LANES].reshape(
            per_step, per_pair, LANES
        )
    meta = meta_scr[pl.ds(pl.multiple_of(step * per_step, per_step), per_step), :]
    meta = jnp.broadcast_to(meta[:, None, :], (per_step, META, LANES)).astype(jnp.bfloat16)
    out_ref[:, (width // LANES) * per_pair :, :] = meta


def best_kernel(per_pair, got_ref, out_ref, x_scr, col_scr, row_scr):
    senders = got_ref.shape[0]
    rows, width = x_scr.shape
    step = pl.program_id(0)
    size = 256

    @pl.when(step == 0)
    def _():
        for c in range(width // LANES):
            x_scr[:, c * LANES : (c + 1) * LANES] = got_ref[:, c * per_pair : (c + 1) * per_pair, :].reshape(
                rows, LANES
            )
        meta = got_ref[:, (width // LANES) * per_pair :, :].astype(jnp.float32)[:, 0:1, :]
        meta = jnp.broadcast_to(meta, (senders, per_pair, LANES)).reshape(rows, LANES)
        own = (iota((rows, LANES), 0) % per_pair) == (iota((rows, LANES), 1) % per_pair)
        meta = jnp.where(own, meta, 0.0).astype(jnp.bfloat16)

        def weights(lane):
            piece = lane // per_pair
            value = jnp.where(piece == 0, 1.0, jnp.where(piece == 1, 256.0, jnp.where(piece == 2, 65536.0, 0.0)))
            return value.astype(jnp.bfloat16)

        col_scr[...] = jnp.dot(meta, weights(iota((LANES, LANES), 0)), preferred_element_type=jnp.float32)
        row_scr[...] = lax.dot_general(
            weights(iota((8, LANES), 1)), meta, (((1,), (1,)), ((), ())), preferred_element_type=jnp.float32
        )

    start = pl.multiple_of(step * size, size)
    mine = x_scr[pl.ds(start, size), :]
    key = row_scr[0:1, pl.ds(start, size)]
    span = float(1 << INDEX_BITS)
    base = jnp.floor(key * (1.0 / span)) * span
    best = jnp.full((1, size), -1.0, jnp.float32)
    chunk = 512
    for j in range(rows // chunk):
        other = x_scr[j * chunk : (j + 1) * chunk, :]
        scores = lax.dot_general(other, mine, (((1,), (1,)), ((), ())), preferred_element_type=jnp.float32)
        col = col_scr[j * chunk : (j + 1) * chunk, :]
        col = jnp.concatenate([col] * (size // LANES), axis=1)
        keep = (col < key) & (col >= base)
        best = jnp.maximum(best, jnp.max(jnp.where(keep, scores, -1.0), axis=0, keepdims=True))
    for b in range(size // LANES):
        out_ref[pl.ds(step * (size // LANES) + b, 1), :] = best[:, b * LANES : (b + 1) * LANES]


def home_kernel(ret_ref, pos_ref, out_ref):
    owners, per_pair = ret_ref.shape
    pos = wide_row(pos_ref)
    rows = pos.shape[1]
    owner = pos // per_pair
    rank = pos - owner * per_pair
    slot = (iota((per_pair, rows), 0) == rank).astype(jnp.bfloat16)
    rest = ret_ref[...]
    spread = jnp.zeros((owners, rows), jnp.float32)
    for _ in range(3):
        part = rest.astype(jnp.bfloat16)
        rest = rest - part.astype(jnp.float32)
        spread = spread + jnp.dot(part, slot, preferred_element_type=jnp.float32)
    mine = jnp.where(iota((owners, rows), 0) == owner, spread, 0.0)
    nearest = jnp.sum(mine, axis=0, keepdims=True)
    for b in range(out_ref.shape[0]):
        out_ref[b : b + 1, :] = nearest[:, b * LANES : (b + 1) * LANES]


def whole(shape):
    return pl.BlockSpec(shape, lambda *_: (0,) * len(shape))


LIMIT = pltpu.CompilerParams(vmem_limit_bytes=48 * 1024 * 1024)


def on_device(embeds, cluster_id, row_index):
    members = lax.axis_size("member")
    rows, width = embeds.shape
    per_owner = CLUSTERS // members
    per_pair = rows // members
    lines = rows // LANES
    tall = width // LANES * per_pair + META
    steps = 4
    payload, pos = pl.pallas_call(
        functools.partial(send_kernel, members, per_owner, per_pair),
        grid=(steps,),
        in_specs=[whole((lines, LANES)), whole((lines, LANES)), whole((rows, width))],
        out_specs=[
            pl.BlockSpec((members // steps, tall, LANES), lambda s: (s, 0, 0)),
            whole((lines, LANES)),
        ],
        out_shape=[
            jax.ShapeDtypeStruct((members, tall, LANES), jnp.bfloat16),
            jax.ShapeDtypeStruct((lines, LANES), jnp.int32),
        ],
        scratch_shapes=[
            pltpu.VMEM((1, rows), jnp.int32),
            pltpu.VMEM((members, LANES), jnp.float32),
        ],
        compiler_params=LIMIT,
        name="send",
    )(cluster_id.reshape(lines, LANES), row_index.reshape(lines, LANES), embeds)
    got = lax.all_to_all(payload, "member", split_axis=0, concat_axis=0, tiled=True)
    best = pl.pallas_call(
        functools.partial(best_kernel, per_pair),
        grid=(rows // 256,),
        in_specs=[whole((members, tall, LANES))],
        out_specs=whole((lines, LANES)),
        out_shape=jax.ShapeDtypeStruct((lines, LANES), jnp.float32),
        scratch_shapes=[
            pltpu.VMEM((rows, width), jnp.bfloat16),
            pltpu.VMEM((rows, LANES), jnp.float32),
            pltpu.VMEM((8, rows), jnp.float32),
        ],
        compiler_params=LIMIT,
        name="best",
    )(got)
    back = lax.all_to_all(best.reshape(members, per_pair), "member", split_axis=0, concat_axis=0, tiled=True)
    nearest = pl.pallas_call(
        home_kernel,
        out_shape=jax.ShapeDtypeStruct((lines, LANES), jnp.float32),
        compiler_params=LIMIT,
        name="home",
    )(back, pos)
    return nearest.reshape(rows)


def solution(mesh):
    in_specs = (P(("outer", "member"), None), P(("outer", "member")), P(("outer", "member")))
    out_specs = P(("outer", "member"))
    return jax.shard_map(
        on_device, mesh=mesh, in_specs=in_specs, out_specs=out_specs, check_vma=False
    )
```

time: 246 us -> 130 us (0.53)
  waiting for transfers between devices: 141 us -> 0 us
  blocking collectives: 15.9 us -> 105 us
  local copies, waits for them, and re-layouts: 39.2 us -> 3.35 us
  starting transfers between devices: 23.7 us -> 0 us
  Pallas kernels: 0 us -> 21.1 us
  other arithmetic: 16.5 us -> 0 us
  matrix products: 9.12 us -> 0 us
    all_to_all x2 -> x0, waiting for transfers between devices: 141 us -> none  [the longest x1 141 us: on_device(): lax.all_to_all(outgoing, 'member', split_axis=0, concat_axis=0, tiled=True)]
    all_to_all x1 -> x2, blocking collectives: 15.9 us -> 105 us  [the longest x1 89.5 us: on_device(): lax.all_to_all(payload, 'member', split_axis=0, concat_axis=0, tiled=True)]
    all_to_all x2 -> x0, starting transfers between devices: 23.7 us -> none  [the longest x1 13.2 us: on_device(): lax.all_to_all(out_order, 'member', split_axis=0, concat_axis=0, tiled=True)]
    pallas_call x0 -> x3, Pallas kernels: none -> 21.1 us  [the longest x1 11 us: on_device(): pl.pallas_call(functools.partial(best_kernel, per_pair), grid=(rows // 25...]
    gather x1 -> x0, local copies, waits for them, and re-layouts: 20.5 us -> none  [on_device(): return returned.reshape(clusters * most)[target]]
    scatter x1 -> x0, other arithmetic: 14.2 us -> none  [on_device(): jnp.zeros((clusters * most, width), jnp.bfloat16).at[target].set(unit)]
    dot_general x4 -> x0, matrix products: 9.12 us -> none  [one(): scores = jnp.dot(flat_rows, flat_rows.T, preferred_element_type=jnp.float32)]
    scatter x1 -> x0, local copies, waits for them, and re-layouts: 8.23 us -> none  [on_device(): jnp.full((clusters * most,), -1, jnp.int32).at[target].set(row_index)]
  transfers between devices with their start and end apart: 2 -> 0, of which waited for: 1 -> 0; matrix products, arithmetic and copies ran while one was open for 6% -> 0% of each run, Pallas kernels for 0% -> 0%
where the time goes in v1:
time: 130 us; the launch traced here: 129 us
  blocking collectives  105 us (81%)
  Pallas kernels  21.1 us (16%)
  local copies, waits for them, and re-layouts  3.35 us (3%)
    all_to_all x1, blocking collectives, on_device(): lax.all_to_all(payload, 'member', split_axis=0, concat_axis=0, tiled=True)  89.5 us
    all_to_all x1, blocking collectives, on_device(): lax.all_to_all(best.reshape(members, per_pair), 'member', split_axis=0, c...  15.3 us
    pallas_call x1, Pallas kernels, on_device(): pl.pallas_call(functools.partial(best_kernel, per_pair), grid=(rows // 25...  11 us
    pallas_call x1, Pallas kernels, on_device(): pl.pallas_call(functools.partial(send_kernel, members, per_owner, per_pai...  9.2 us
    unnamed x6, local copies, waits for them, and re-layouts  3.28 us

profile of v1, /device:TPU:1, one launch (start us, length us, event | category | flops | bytes accessed | tf_op | source)
XLA Modules:
  0.0 129.2 jit_solution(13845056997652556071)
XLA Ops:
  0.0 0.0 copy-start
  0.0 1.9 %copy-done = bf16[2048,768]{1,0:T(8,128)(2,1)S(1)} copy-done((bf16[2048,768]{1,0:T(8,128)(2,1)S(1)}, bf16[2048,768]{1,0:T(8,128)(2,1)}, u32[]{:S(2)}) %copy-start) | copy-done | bytes 3145752
  1.9 0.0 copy-start.1
  1.9 0.7 copy-done.1
  2.6 0.0 copy-start.2
  2.6 0.7 copy-done.2
  3.3 9.2 %send.1 = (bf16[64,200,128]{2,1,0:T(8,128)(2,1)}, s32[16,128]{1,0:T(8,128)S(1)}) custom-call(s32[16,128]{1,0:T(8,128)S(1)} %bitcast.6, s32[16,128]{1,0:T(8,128)S(1)} %bitcast.7, bf16[2048,768]{1,0:T(8,128)(2,1)S(1)} %copy-done), custom_call_target="tpu_custom_call" | custom-call | tf_op jit(solution)/shard_map/send/pallas_call | solution.py:154
  12.5 89.5 %all_to_all.16.got_ref = bf16[64,200,128]{2,1,0:T(8,128)(2,1)S(1)} all-to-all(bf16[64,200,128]{2,1,0:T(8,128)(2,1)} %get-tuple-element.7), channel_id=1, replica_groups=mesh['outer'=4,'member'=64] {'member'}, dimensions={0} | all-to-all | bytes 6553600 | tf_op jit(solution)/shard_map/all_to_all | solution.py:173
  102.0 11.0 %best.1 = f32[16,128]{1,0:T(8,128)S(1)} custom-call(bf16[64,200,128]{2,1,0:T(8,128)(2,1)S(1)} %all_to_all.16.got_ref), custom_call_target="tpu_custom_call" | custom-call | tf_op jit(solution)/shard_map/best/pallas_call | solution.py:174
  112.9 0.1 all_to_all.11
  113.0 15.3 %all_to_all.17 = f32[64,1,32]{2,1,0:T(1,128)S(1)} all-to-all(f32[64,1,32]{2,1,0:T(1,128)S(1)} %bitcast.8), channel_id=1, replica_groups=mesh['outer'=4,'member'=64] {'member'}, dimensions={0} | all-to-all | bytes 16384 | tf_op jit(solution)/shard_map/all_to_all | solution.py:188
  128.3 1.0 home.1
Async XLA Ops:
  0.0 1.9 %copy-start = (bf16[2048,768]{1,0:T(8,128)(2,1)S(1)}, bf16[2048,768]{1,0:T(8,128)(2,1)}, u32[]{:S(2)}) copy-start(bf16[2048,768]{1,0:T(8,128)(2,1)} %emb_ref.1) | copy-start | bytes 9437188
  1.9 0.7 copy-start.1
  2.6 0.7 copy-start.2

commit v2 on v0

v2 whole, which is shorter than its diff:
```python
import functools

import jax
import jax.numpy as jnp
from jax import lax
from jax.experimental import pallas as pl
from jax.experimental.pallas import tpu as pltpu
from jax.sharding import PartitionSpec as P

CLUSTERS = 256
INDEX_BITS = 17
LANES = 128
META = 8
TILE = 256
NZ, CORES, PLANE = 8, 2, 8
EARLY = (4, 3, 5, 0)
LATE = (2, 6, 1, 7)
ORDER = EARLY + LATE
BF16, F32, I32 = jnp.bfloat16, jnp.float32, jnp.int32


def iota(shape, dim):
    return lax.broadcasted_iota(I32, shape, dim)


def dot(a, b):
    return jnp.dot(a, b, preferred_element_type=F32)


def dot_t(a, b):
    return lax.dot_general(a, b, (((1,), (1,)), ((), ())), preferred_element_type=F32)


def wide_row(ref):
    return jnp.concatenate([ref[b : b + 1, :] for b in range(ref.shape[0])], axis=1)


def put_row(ref, row):
    for b in range(ref.shape[0]):
        ref[b : b + 1, :] = row[:, b * LANES : (b + 1) * LANES]


def my_z():
    return (lax.axis_index("member") // CORES) % NZ


def shift_plane(owner):
    dz = ((owner // CORES) % NZ + NZ - my_z()) % NZ
    return dz, owner // (CORES * NZ) * CORES + owner % CORES


def route(owners, per_owner, per_pair, cid, idx):
    rows = cid.shape[1]
    owner = cid // per_owner
    dz, plane = shift_plane(owner)
    hot = (iota((owners, rows), 0) == dz * PLANE + plane).astype(BF16)
    before = (iota((TILE, TILE), 0) < iota((TILE, TILE), 1)).astype(BF16)
    carry = jnp.zeros((owners, 1), F32)
    ranks = []
    for b in range(rows // TILE):
        part = hot[:, b * TILE : (b + 1) * TILE]
        wide = part.astype(F32)
        ranks.append(jnp.sum((dot(part, before) + carry) * wide, axis=0, keepdims=True))
        carry = carry + jnp.sum(wide, axis=1, keepdims=True)
    rank = jnp.concatenate(ranks, axis=1).astype(I32)
    key = (cid - owner * per_owner) * (1 << INDEX_BITS) + idx
    slot = iota((per_pair, rows), 0) == rank
    pieces = (key & 255, (key >> 8) & 255, key >> 16)
    spread = [jnp.where(slot, p.astype(F32), 0.0).astype(BF16) for p in pieces]
    spread.append(jnp.zeros((LANES - 3 * per_pair, rows), BF16))
    meta = dot_t(hot, jnp.concatenate(spread, axis=0))
    return owner * per_pair + rank, meta


def place(pos, per_pair, shifts, inner):
    owner = pos // per_pair
    rank = pos - owner * per_pair
    dz, plane = shift_plane(owner)
    goal = jnp.full(pos.shape, -1, I32)
    for k, shift in enumerate(shifts):
        slot = plane * len(shifts) + k if inner else k * PLANE + plane
        goal = jnp.where(dz == shift, slot * per_pair + rank, goal)
    return goal


def unit_rows(goal, first, size, emb):
    pick = (iota((size, emb.shape[0]), 0) + first == goal).astype(BF16)
    moved = dot(pick, emb)
    inverse = lax.rsqrt(jnp.sum(moved * moved, axis=1, keepdims=True) + 1e-06)
    return (moved * inverse).astype(BF16)


def pack(unit, meta, per_pair):
    blocks = unit.shape[0] // per_pair
    parts = [
        unit[:, c * LANES : (c + 1) * LANES].reshape(blocks, per_pair, LANES)
        for c in range(unit.shape[1] // LANES)
    ]
    parts.append(jnp.broadcast_to(meta[:, None, :], (blocks, META, LANES)).astype(BF16))
    return parts


def put_parts(ref, parts):
    at = 0
    for part in parts:
        ref[..., at : at + part.shape[-2], :] = part
        at += part.shape[-2]


def first_kernel(
    owners, per_owner, per_pair, cid_hbm, idx_hbm, emb_hbm, out_ref, pos_ref, meta_ref, flag_ref,
    cid_ref, idx_ref, emb_ref, sem
):
    copies = [
        pltpu.make_async_copy(src, dst, sem.at[n])
        for n, (src, dst) in enumerate(((cid_hbm, cid_ref), (idx_hbm, idx_ref), (emb_hbm, emb_ref)))
    ]
    for copy in copies:
        copy.start()
    copies[0].wait()
    copies[1].wait()
    pos, meta = route(owners, per_owner, per_pair, wide_row(cid_ref), wide_row(idx_ref))
    put_row(pos_ref, pos)
    meta_ref[...] = meta
    flag_ref[0] = 1
    copies[2].wait()
    unit = unit_rows(place(pos, per_pair, EARLY[:1], False), 0, PLANE * per_pair, emb_ref[...])
    shift = EARLY[0]
    put_parts(out_ref, pack(unit, meta[shift * PLANE : (shift + 1) * PLANE], per_pair))


def some_kernel(per_pair, shifts, pos_ref, meta_ref, emb_hbm, *refs):
    *outs, emb_ref, sem = refs
    copy = pltpu.make_async_copy(emb_hbm, emb_ref, sem)
    copy.start()
    goal = place(wide_row(pos_ref), per_pair, shifts, False)
    copy.wait()
    size = PLANE * per_pair
    unit = unit_rows(goal, 0, size * len(outs), emb_ref[...])
    for k, (shift, out_ref) in enumerate(zip(shifts, outs)):
        meta = meta_ref[shift * PLANE : (shift + 1) * PLANE, :]
        put_parts(out_ref, pack(unit[k * size : (k + 1) * size], meta, per_pair))


def late_kernel(per_pair, pos_ref, meta_ref, emb_hbm, out_ref, emb_ref, goal_scr, sem):
    step = pl.program_id(0)
    per_step = out_ref.shape[0]
    size = per_step * len(LATE) * per_pair

    @pl.when(step == 0)
    def _():
        copy = pltpu.make_async_copy(emb_hbm, emb_ref, sem)
        copy.start()
        goal_scr[...] = place(wide_row(pos_ref), per_pair, LATE, True)
        copy.wait()

    unit = unit_rows(goal_scr[...], step * size, size, emb_ref[...])
    for p in range(per_step):
        for k, shift in enumerate(LATE):
            at = (p * len(LATE) + k) * per_pair
            meta = meta_ref[pl.ds(shift * PLANE + step * per_step + p, 1), :]
            parts = pack(unit[at : at + per_pair], meta, per_pair)
            put_parts(out_ref.at[p, k], [part[0] for part in parts])


def piece_weights(lane, per_pair):
    piece = lane // per_pair
    value = jnp.where(piece == 0, 1.0, jnp.where(piece == 1, 256.0, jnp.where(piece == 2, 65536.0, 0.0)))
    return value.astype(BF16)


def best_kernel(per_pair, early_ref, *refs):
    *late, out_ref, col_scr, base_scr, row_scr, across_scr = refs
    rows = col_scr.shape[0]
    blocks = [early_ref.at[:, k] for k in range(len(EARLY))] + list(late)
    chunks = early_ref.shape[2] // per_pair
    span = float(1 << INDEX_BITS)

    def tile(t):
        return jnp.concatenate(
            [blocks[t][:, c * per_pair : (c + 1) * per_pair, :].reshape(TILE, LANES) for c in range(chunks)], axis=1
        )

    meta = [block[:, chunks * per_pair :, :].astype(F32)[:, 0:1, :] for block in blocks]
    meta = jnp.concatenate(meta, axis=0)
    meta = jnp.broadcast_to(meta, (rows // per_pair, per_pair, LANES)).reshape(rows, LANES)
    own = (iota((rows, LANES), 0) % per_pair) == (iota((rows, LANES), 1) % per_pair)
    meta = jnp.where(own, meta, 0.0).astype(BF16)
    col = dot(meta, piece_weights(iota((LANES, LANES), 0), per_pair))
    col_scr[...] = col
    base_scr[...] = jnp.floor(col * (1.0 / span)) * span
    row_scr[...] = dot_t(piece_weights(iota((8, LANES), 1), per_pair), meta)
    across_scr[...] = jnp.full(across_scr.shape, -1.0, F32)

    down = []
    for i in range(rows // TILE):
        mine = tile(i)
        row = [row_scr[0:1, i * TILE + b : i * TILE + b + LANES] for b in range(0, TILE, LANES)]
        base = [jnp.floor(r * (1.0 / span)) * span for r in row]
        best = [jnp.full((1, LANES), -1.0, F32) for _ in row]
        for j in range(i + 1):
            at = slice(j * TILE, (j + 1) * TILE)
            scores = dot_t(tile(j), mine)
            col, low = col_scr[at, :], base_scr[at, :]
            across = across_scr[at, :]
            for b in range(len(row)):
                part = scores[:, b * LANES : (b + 1) * LANES]
                kept = jnp.where((col < row[b]) & (col >= base[b]), part, -1.0)
                best[b] = jnp.maximum(best[b], jnp.max(kept, axis=0, keepdims=True))
                if j < i:
                    across = jnp.maximum(across, jnp.where((row[b] < col) & (row[b] >= low), part, -1.0))
            if j < i:
                across_scr[at, :] = across
        down += best

    best = [
        jnp.maximum(
            down[b], jnp.max(across_scr[b * LANES : (b + 1) * LANES, :].T, axis=0, keepdims=True)
        )
        for b in range(rows // LANES)
    ]
    best = jnp.concatenate(best, axis=1)
    homes = out_ref.shape[0]
    place_in = iota((1, rows), 1)
    slot = place_in // TILE
    plane = place_in % TILE // per_pair
    shift = jnp.zeros((1, rows), I32)
    for t, dz in enumerate(ORDER):
        shift = jnp.where(slot == t, dz, shift)
    z = (my_z() + NZ - shift) % NZ
    home = plane // CORES * (CORES * NZ) + z * CORES + plane % CORES
    to = (iota((homes, rows), 0) == home).astype(BF16)
    own = iota((per_pair, rows), 0) == place_in % per_pair
    rest = jnp.where(own, best, 0.0)
    total = jnp.zeros(out_ref.shape, F32)
    for _ in range(3):
        part = rest.astype(BF16)
        rest = rest - part.astype(F32)
        total = total + dot_t(to, part)
    out_ref[...] = total


def home_kernel(ret_ref, pos_ref, out_ref):
    owners, per_pair = ret_ref.shape
    pos = wide_row(pos_ref)
    rows = pos.shape[1]
    owner = pos // per_pair
    rank = pos - owner * per_pair
    slot = (iota((per_pair, rows), 0) == rank).astype(BF16)
    rest = ret_ref[...]
    spread = jnp.zeros((owners, rows), F32)
    for _ in range(3):
        part = rest.astype(BF16)
        rest = rest - part.astype(F32)
        spread = spread + dot(part, slot)
    mine = jnp.where(iota((owners, rows), 0) == owner, spread, 0.0)
    put_row(out_ref, jnp.sum(mine, axis=0, keepdims=True))


def whole(shape):
    return pl.BlockSpec(shape, lambda *_: (0,) * len(shape))


ANY = pl.BlockSpec(memory_space=pl.ANY)
FIRST = pltpu.CompilerParams(vmem_limit_bytes=61 * 1024 * 1024)
LIMIT = pltpu.CompilerParams(vmem_limit_bytes=24 * 1024 * 1024)


def shape(dims, dtype):
    return jax.ShapeDtypeStruct(dims, dtype)


def cost(macs):
    return pl.CostEstimate(flops=2 * macs, bytes_accessed=8 << 20, transcendentals=0)


def to_shift(rows, dz):
    members = lax.axis_size("member")
    pairs = []
    for i in range(members):
        z = (i // CORES) % NZ
        pairs.append((i, i + ((z + dz) % NZ - z) * CORES))
    return lax.ppermute(rows, "member", pairs)


def in_plane(rows):
    members = lax.axis_size("member")
    groups = [[i for i in range(members) if (i // CORES) % NZ == z] for z in range(NZ)]
    return lax.all_to_all(rows, "member", split_axis=0, concat_axis=0, tiled=True, axis_index_groups=groups)


def step_of_its_own(run, flag, *args):
    kinds = jax.eval_shape(run, *args)
    skip = lambda *_: jax.tree.map(lambda kind: jnp.zeros(kind.shape, kind.dtype), kinds)
    return lax.cond(flag[0] > 0, run, skip, *args)


def on_device(embeds, cluster_id, row_index):
    members = lax.axis_size("member")
    rows, width = embeds.shape
    per_owner = CLUSTERS // members
    per_pair = rows // members
    lines = rows // LANES
    tall = width // LANES * per_pair + META
    block = (PLANE, tall, LANES)
    one, pos, meta, flag = pl.pallas_call(
        functools.partial(first_kernel, members, per_owner, per_pair),
        in_specs=[ANY, ANY, ANY],
        out_specs=[whole(block), whole((lines, LANES)), whole((members, LANES)), pl.BlockSpec(memory_space=pltpu.SMEM)],
        out_shape=[
            shape(block, BF16),
            shape((lines, LANES), I32),
            shape((members, LANES), F32),
            shape((1,), I32),
        ],
        scratch_shapes=[
            pltpu.VMEM((lines, LANES), I32),
            pltpu.VMEM((lines, LANES), I32),
            pltpu.VMEM((rows, width), BF16),
            pltpu.SemaphoreType.DMA((3,)),
        ],
        compiler_params=FIRST,
        cost_estimate=cost(TILE * rows * width),
        name="send_first",
    )(cluster_id.reshape(lines, LANES), row_index.reshape(lines, LANES), embeds)
    got = [to_shift(one, EARLY[0])]

    def send_some(shifts, name, pos, meta, embeds):
        return pl.pallas_call(
            functools.partial(some_kernel, per_pair, shifts),
            in_specs=[whole((lines, LANES)), whole((members, LANES)), ANY],
            out_shape=[shape(block, BF16) for _ in shifts],
            scratch_shapes=[pltpu.VMEM((rows, width), BF16), pltpu.SemaphoreType.DMA],
            compiler_params=LIMIT,
            cost_estimate=cost(len(shifts) * TILE * rows * width),
            name=name,
        )(pos, meta, embeds)

    more = send_some(EARLY[1:-1], "send_early", pos, meta, embeds)
    got += [to_shift(x, dz) for x, dz in zip(more, EARLY[1:-1])]

    def late_part(pos, meta, embeds):
        steps = 4
        late = pl.pallas_call(
            functools.partial(late_kernel, per_pair),
            grid=(steps,),
            in_specs=[whole((lines, LANES)), whole((members, LANES)), ANY],
            out_specs=pl.BlockSpec((PLANE // steps, len(LATE), tall, LANES), lambda s: (s, 0, 0, 0)),
            out_shape=shape((PLANE, len(LATE), tall, LANES), BF16),
            scratch_shapes=[
                pltpu.VMEM((rows, width), BF16),
                pltpu.VMEM((1, rows), I32),
                pltpu.SemaphoreType.DMA,
            ],
            compiler_params=LIMIT,
            cost_estimate=cost(len(LATE) * TILE * rows * width),
            name="send_late",
        )(pos, meta, embeds)
        late = in_plane(late)
        return [late[:, k] for k in range(len(LATE))] + list(
            send_some(EARLY[-1:], "send_own", pos, meta, embeds)
        )

    *moving, own = step_of_its_own(late_part, flag, pos, meta, embeds)
    shifted = [to_shift(x, dz) for x, dz in zip(moving, LATE)]
    early = step_of_its_own(lambda *got: in_plane(jnp.stack(got, axis=1)), flag, *got, own)
    best = pl.pallas_call(
        functools.partial(best_kernel, per_pair),
        out_shape=shape((members, per_pair), F32),
        scratch_shapes=[
            pltpu.VMEM((rows, LANES), F32),
            pltpu.VMEM((rows, LANES), F32),
            pltpu.VMEM((8, rows), F32),
            pltpu.VMEM((rows, LANES), F32),
        ],
        compiler_params=LIMIT,
        cost_estimate=cost(rows * rows * width // 2),
        name="best",
    )(early, *shifted)
    back = lax.all_to_all(best, "member", split_axis=0, concat_axis=0, tiled=True)
    nearest = pl.pallas_call(
        home_kernel,
        out_shape=shape((lines, LANES), F32),
        compiler_params=LIMIT,
        name="home",
    )(back, pos)
    return nearest.reshape(rows)


def solution(mesh):
    in_specs = (P(("outer", "member"), None), P(("outer", "member")), P(("outer", "member")))
    out_specs = P(("outer", "member"))
    return jax.shard_map(
        on_device, mesh=mesh, in_specs=in_specs, out_specs=out_specs, check_vma=False
    )
```

time: 246 us -> 114 us (0.46)
  waiting for transfers between devices: 141 us -> 18.5 us
  local copies, waits for them, and re-layouts: 39.2 us -> 2.85 us
  Pallas kernels: 0 us -> 25.7 us
  blocking collectives: 15.9 us -> 40.3 us
  other arithmetic: 16.5 us -> 1.33 us
  matrix products: 9.12 us -> 0 us
    all_to_all x2 -> x1, waiting for transfers between devices: 141 us -> 18.4 us  [in_plane(): lax.all_to_all(rows, 'member', split_axis=0, concat_axis=0, tiled=True, a...]
    pallas_call x0 -> x6, Pallas kernels: none -> 25.7 us  [the longest x1 8.28 us: on_device(): pl.pallas_call(functools.partial(best_kernel, per_pair), out_shape=shape(...]
    all_to_all x1 -> x2, blocking collectives: 15.9 us -> 40.3 us  [the longest x1 26.9 us: in_plane(): lax.all_to_all(rows, 'member', split_axis=0, concat_axis=0, tiled=True, a...]
    gather x1 -> x0, local copies, waits for them, and re-layouts: 20.5 us -> none  [on_device(): return returned.reshape(clusters * most)[target]]
    ppermute x0 -> x7, starting transfers between devices: none -> 18.6 us  [to_shift(): return lax.ppermute(rows, 'member', pairs)]
    all_to_all x2 -> x1, starting transfers between devices: 23.7 us -> 5.99 us  [in_plane(): lax.all_to_all(rows, 'member', split_axis=0, concat_axis=0, tiled=True, a...]
    scatter x1 -> x0, other arithmetic: 14.2 us -> none  [on_device(): jnp.zeros((clusters * most, width), jnp.bfloat16).at[target].set(unit)]
    dot_general x4 -> x0, matrix products: 9.12 us -> none  [one(): scores = jnp.dot(flat_rows, flat_rows.T, preferred_element_type=jnp.float32)]
  transfers between devices with their start and end apart: 2 -> 8, of which waited for: 1 -> 1; matrix products, arithmetic and copies ran while one was open for 6% -> 2% of each run, Pallas kernels for 0% -> 11%
where the time goes in v2:
time: 114 us
  blocking collectives  40.3 us (35%)
  Pallas kernels  25.7 us (23%)
  starting transfers between devices  24.6 us (22%)
  waiting for transfers between devices  18.5 us (16%)
  local copies, waits for them, and re-layouts  2.85 us (2%)
  other arithmetic  1.33 us (1%)
    all_to_all x1, blocking collectives, in_plane(): lax.all_to_all(rows, 'member', split_axis=0, concat_axis=0, tiled=True, a...  26.9 us
    ppermute x7, starting transfers between devices, to_shift(): return lax.ppermute(rows, 'member', pairs)  18.6 us
    all_to_all x1, waiting for transfers between devices, in_plane(): lax.all_to_all(rows, 'member', split_axis=0, concat_axis=0, tiled=True, a...  18.4 us
    all_to_all x1, blocking collectives, on_device(): lax.all_to_all(best, 'member', split_axis=0, concat_axis=0, tiled=True)  13.4 us
    pallas_call x1, Pallas kernels, on_device(): pl.pallas_call(functools.partial(best_kernel, per_pair), out_shape=shape(...  8.28 us
    pallas_call x2, Pallas kernels, send_some(): pl.pallas_call(functools.partial(some_kernel, per_pair, shifts), in_specs...  6.92 us
    all_to_all x1, starting transfers between devices, in_plane(): lax.all_to_all(rows, 'member', split_axis=0, concat_axis=0, tiled=True, a...  5.99 us
    pallas_call x1, Pallas kernels, late_part(): pl.pallas_call(functools.partial(late_kernel, per_pair), grid=(steps,), i...  5.54 us
  transfers between devices with their start and end apart: 8, of which 1 were waited for; matrix products, arithmetic and copies ran while one was open for 2% of the time, Pallas kernels for 11%

profile of v2, /device:TPU:1, one launch (start us, length us, event | category | flops | bytes accessed | tf_op | source)
XLA Modules:
  0.0 114.0 jit_solution(207021143585849994)
XLA Ops:
  0.0 4.0 %send_first.1 = (bf16[8,200,128]{2,1,0:T(8,128)(2,1)}, s32[16,128]{1,0:T(8,128)S(1)}, f32[64,128]{1,0:T(8,128)S(1)}, s32[1]{0:T(128)}) custom-call(s32[16,128]{1,0:T(8,128)} %bitcast.24, s32[16,128]{1,0:T(8,128)} %bitcast.25, bf16[2048,768]{1,0:T(8,128)(2,1)} %emb_hbm.3), custom_call_target="tpu_custom_call" | custom-call | flops 805306368 | bytes 8388608 | tf_op jit(solution)/shard_map/send_first/pallas_call | solution.py:306
  4.0 7.8 %collective-permute-start = (bf16[8,200,128]{2,1,0:T(8,128)(2,1)}, bf16[8,200,128]{2,1,0:T(8,128)(2,1)S(1)}, u32[]{:S(2)}, u32[]{:S(2)}) collective-permute-start(bf16[8,200,128]{2,1,0:T(8,128)(2,1)} %get-tuple-element.41), channel_id=1, source_target_pairs={{0,8},{1,9},{2,10},{3,11},{4,12},{5,13},{6,14},{7,15},{8,0},{9,1},... | collective-permute-start | bytes 1228808 | tf_op jit(solution)/shard_map/ppermute | solution.py:283
  11.8 4.0 %send_early.1 = (bf16[8,200,128]{2,1,0:T(8,128)(2,1)S(1)}, bf16[8,200,128]{2,1,0:T(8,128)(2,1)S(1)}) custom-call(s32[16,128]{1,0:T(8,128)S(1)} %get-tuple-element.42.pos_ref, f32[64,128]{1,0:T(8,128)S(1)} %get-tuple-element.43.meta_ref, bf16[2048,768]{1,0:T(8,128)(2,1)} %emb_hbm.3), custom_call_target="tpu_custom_call" | custom-call | flops 1610612736 | bytes 8388608 | tf_op jit(solution)/shard_map/send_early/pallas_call | solution.py:329
  15.8 1.7 %collective-permute-start.1 = (bf16[8,200,128]{2,1,0:T(8,128)(2,1)S(1)}, bf16[8,200,128]{2,1,0:T(8,128)(2,1)}, u32[]{:S(2)}, u32[]{:S(2)}) collective-permute-start(bf16[8,200,128]{2,1,0:T(8,128)(2,1)S(1)} %get-tuple-element.44), channel_id=1, source_target_pairs={{0,6},{1,7},{2,8},{3,9},{4,10},{5,11},{6,12},{7,13},{8,14},{9,15},... | collective-permute-start | bytes 1228808 | tf_op jit(solution)/shard_map/ppermute | solution.py:283
  17.5 2.8 %collective-permute-start.2 = (bf16[8,200,128]{2,1,0:T(8,128)(2,1)S(1)}, bf16[8,200,128]{2,1,0:T(8,128)(2,1)}, u32[]{:S(2)}, u32[]{:S(2)}) collective-permute-start(bf16[8,200,128]{2,1,0:T(8,128)(2,1)S(1)} %get-tuple-element.45), channel_id=1, source_target_pairs={{0,10},{1,11},{2,12},{3,13},{4,14},{5,15},{6,0},{7,1},{8,2},{9,3},... | collective-permute-start | bytes 1228808 | tf_op jit(solution)/shard_map/ppermute | solution.py:283
  21.0 35.8 %conditional.2 = (bf16[8,200,128]{2,1,0:T(8,128)(2,1)}, bf16[8,200,128]{2,1,0:T(8,128)(2,1)}, bf16[8,200,128]{2,1,0:T(8,128)(2,1)}, bf16[8,200,128]{2,1,0:T(8,128)(2,1)}, bf16[8,200,128]{2,1,0:T(8,128)(2,1)S(1)}) conditional(s32[]{:T(128)} %bitcast.10, () %tuple.20, (s32[16,128]{1,0:T(8,128)S(1)}, f32[64,128]{1,0:T(8,128)S(1)}, ...), branch_computations={%region_0.0_spmd, %region_1.0_spmd} | conditional | flops 4026531840 | bytes 37552228 | solution.py:295
  21.0 1.6 %copy-done.1 = bf16[2048,768]{1,0:T(8,128)(2,1)} copy-done((bf16[2048,768]{1,0:T(8,128)(2,1)}, bf16[2048,768]{1,0:T(8,128)(2,1)S(1)}, u32[]{:S(2)}) %copy-start.1) | copy-done | bytes 3145752 | tf_op jit(solution)/shard_map/cond
  22.7 5.5 %send_late.1 = bf16[8,4,200,128]{3,2,1,0:T(8,128)(2,1)} custom-call(s32[16,128]{1,0:T(8,128)S(1)} %get-tuple-element.22.pos_ref, f32[64,128]{1,0:T(8,128)S(1)} %get-tuple-element.23.meta_ref, bf16[2048,768]{1,0:T(8,128)(2,1)S(1)} %get-tuple-element.24.emb_hbm), custom_call_target="tpu_custom_call" | custom-call | flops 3221225472 | bytes 8388608 | tf_op jit(solution)/shard_map/cond/branch_1_fun/send_late/pallas_call | solution.py:344
  28.2 6.0 %all-to-all-start = ((bf16[8,4,200,128]{3,2,1,0:T(8,128)(2,1)}), bf16[8,4,200,128]{3,2,1,0:T(8,128)(2,1)S(1)}, u32[]{:S(2)}, u32[]{:S(2)}) async-start(bf16[8,4,200,128]{3,2,1,0:T(8,128)(2,1)} %send_late.1), calls=%async_computation | async-start | bytes 3276800 | tf_op jit(solution)/shard_map/cond/branch_1_fun/all_to_all | solution.py:289
  34.2 3.0 %send_own.1 = bf16[8,200,128]{2,1,0:T(8,128)(2,1)S(1)} custom-call(s32[16,128]{1,0:T(8,128)S(1)} %get-tuple-element.22.pos_ref, f32[64,128]{1,0:T(8,128)S(1)} %get-tuple-element.23.meta_ref, bf16[2048,768]{1,0:T(8,128)(2,1)} %copy-done.1), custom_call_target="tpu_custom_call" | custom-call | flops 805306368 | bytes 8388608 | tf_op jit(solution)/shard_map/cond/branch_1_fun/send_own/pallas_call | solution.py:329
  37.2 18.4 %all-to-all-done = bf16[8,4,200,128]{3,2,1,0:T(8,128)(2,1)S(1)} async-done(((bf16[8,4,200,128]{3,2,1,0:T(8,128)(2,1)}), bf16[8,4,200,128]{3,2,1,0:T(8,128)(2,1)S(1)}, u32[]{:S(2)}, u32[]{:S(2)}) %all-to-all-start) | async-done | bytes 1638432 | tf_op jit(solution)/shard_map/cond/branch_1_fun/all_to_all | solution.py:289
  55.6 1.2 %slice_bitcast_fusion = (bf16[8,200,128]{2,1,0:T(8,128)(2,1)}, bf16[8,200,128]{2,1,0:T(8,128)(2,1)}, bf16[8,200,128]{2,1,0:T(8,128)(2,1)}, bf16[8,200,128]{2,1,0:T(8,128)(2,1)}) fusion(bf16[8,4,200,128]{3,2,1,0:T(8,128)(2,1)S(1)} %all-to-all-done), kind=kLoop, calls=%fused_computation | loop fusion | bytes 3276800 | tf_op jit(solution)/shard_map/cond/branch_1_fun/squeeze | solution.py:360
  56.8 1.3 %collective-permute-start.3 = (bf16[8,200,128]{2,1,0:T(8,128)(2,1)}, bf16[8,200,128]{2,1,0:T(8,128)(2,1)S(1)}, u32[]{:S(2)}, u32[]{:S(2)}) collective-permute-start(bf16[8,200,128]{2,1,0:T(8,128)(2,1)} %get-tuple-element.47), channel_id=1, source_target_pairs={{0,4},{1,5},{2,6},{3,7},{4,8},{5,9},{6,10},{7,11},{8,12},{9,13},{1... | collective-permute-start | bytes 1228808 | tf_op jit(solution)/shard_map/ppermute | solution.py:283
  58.1 2.3 %collective-permute-start.4 = (bf16[8,200,128]{2,1,0:T(8,128)(2,1)}, bf16[8,200,128]{2,1,0:T(8,128)(2,1)S(1)}, u32[]{:S(2)}, u32[]{:S(2)}) collective-permute-start(bf16[8,200,128]{2,1,0:T(8,128)(2,1)} %get-tuple-element.48), channel_id=1, source_target_pairs={{0,12},{1,13},{2,14},{3,15},{4,0},{5,1},{6,2},{7,3},{8,4},{9,5},{1... | collective-permute-start | bytes 1228808 | tf_op jit(solution)/shard_map/ppermute | solution.py:283
  60.4 0.0 collective-permute-done
  60.4 0.8 collective-permute-start.5
  61.3 1.8 %collective-permute-start.6 = (bf16[8,200,128]{2,1,0:T(8,128)(2,1)}, bf16[8,200,128]{2,1,0:T(8,128)(2,1)S(1)}, u32[]{:S(2)}, u32[]{:S(2)}) collective-permute-start(bf16[8,200,128]{2,1,0:T(8,128)(2,1)} %get-tuple-element.50), channel_id=1, source_target_pairs={{0,14},{1,15},{2,0},{3,1},{4,2},{5,3},{6,4},{7,5},{8,6},{9,7},{10,... | collective-permute-start | bytes 1228808 | tf_op jit(solution)/shard_map/ppermute | solution.py:283
  63.1 28.2 %conditional.3 = (bf16[8,4,200,128]{3,2,1,0:T(8,128)(2,1)}) conditional(s32[]{:T(128)} %bitcast.10, () %tuple.19, (bf16[8,200,128]{2,1,0:T(8,128)(2,1)S(1)}, bf16[8,200,128]{2,1,0:T(8,128)(2,1)}, bf16[8,200,128]{2,1,0:T(8,128)(2,1)}, bf16[8,200,128]{2,1,0:T(8,128)(2,1)S(1)}) %tuple.22), branch_computations={%region_2.0_spmd, %region_3.0_spmd} | conditional | flops 2457600 | bytes 6553608 | solution.py:295
  63.1 1.3 %pad_maximum_fusion = bf16[8,4,200,128]{3,2,1,0:T(8,128)(2,1)S(1)} fusion(bf16[8,1,200,128]{3,2,1,0:T(8,128)(2,1)S(1)} %bitcast.22, bf16[8,1,200,128]{3,2,1,0:T(8,128)(2,1)} %bitcast.6, bf16[8,1,200,128]{3,2,1,0:T(8,128)(2,1)} %bitcast.5, bf16[8,1,200,128]{3,2,1,0:T(8,128)(2,1)S(1)} %bitcast.23), kind=kLoop, calls=%fused_computation.4 | loop fusion | flops 2457600 | bytes 3276800 | tf_op jit(solution)/shard_map/cond/branch_1_fun/stack | solution.py:366
  64.4 26.9 %all_to_all.19 = bf16[8,4,200,128]{3,2,1,0:T(8,128)(2,1)} all-to-all(bf16[8,4,200,128]{3,2,1,0:T(8,128)(2,1)S(1)} %pad_maximum_fusion), channel_id=1, replica_groups={{0,1,16,17,32,33,48,49},{2,3,18,19,34,35,50,51},{4,5,20,21,36,37,52,53}..., dimensions={0} | all-to-all | bytes 3276800 | tf_op jit(solution)/shard_map/cond/branch_1_fun/all_to_all | solution.py:289
  91.3 0.0 collective-permute-done.3.refs_0_
  91.3 8.3 %best.1 = f32[64,32]{1,0:T(8,128)S(1)} custom-call(bf16[8,4,200,128]{3,2,1,0:T(8,128)(2,1)} %get-tuple-element.65.early_ref, bf16[8,200,128]{2,1,0:T(8,128)(2,1)S(1)} %collective-permute-done.3.refs_0_, bf16[8,200,128]{2,1,0:T(8,128)(2,1)S(1)} %collective-permute-done.4.refs_1_, bf16[8,200,128]{2,1,0:T(8,128)(2,1)S(1)} %collective-permute-done.5.refs_2_, ...), custom_call_target="tpu_custom_call" | custom-call | flops 3221225472 | bytes 8388608 | tf_op jit(solution)/shard_map/best/pallas_call | solution.py:367
  99.6 13.4 %all_to_all.20 = f32[64,1,32]{2,1,0:T(1,128)S(1)} all-to-all(f32[64,1,32]{2,1,0:T(1,128)S(1)} %bitcast.21), channel_id=1, replica_groups=mesh['outer'=4,'member'=64] {'member'}, dimensions={0} | all-to-all | bytes 16384 | tf_op jit(solution)/shard_map/all_to_all | solution.py:380
  113.0 1.0 home.1
  (8 shorter events, 0.0 us)
Async XLA Ops:
  4.0 56.4 %collective-permute-start = (bf16[8,200,128]{2,1,0:T(8,128)(2,1)}, bf16[8,200,128]{2,1,0:T(8,128)(2,1)S(1)}, u32[]{:S(2)}, u32[]{:S(2)}) collective-permute-start(bf16[8,200,128]{2,1,0:T(8,128)(2,1)} %get-tuple-element.41), channel_id=1, source_target_pairs={{0,8},{1,9},{2,10},{3,11},{4,12},{5,13},{6,14},{7,15},{8,0},{9,1},... | collective-permute-start | bytes 1228808 | tf_op jit(solution)/shard_map/ppermute | solution.py:283
  11.8 9.2 %copy-start = (bf16[2048,768]{1,0:T(8,128)(2,1)S(1)}, bf16[2048,768]{1,0:T(8,128)(2,1)}, u32[]{:S(2)}) copy-start(bf16[2048,768]{1,0:T(8,128)(2,1)} %emb_hbm.3) | copy-start | bytes 9437188
  15.8 45.5 %collective-permute-start.1 = (bf16[8,200,128]{2,1,0:T(8,128)(2,1)S(1)}, bf16[8,200,128]{2,1,0:T(8,128)(2,1)}, u32[]{:S(2)}, u32[]{:S(2)}) collective-permute-start(bf16[8,200,128]{2,1,0:T(8,128)(2,1)S(1)} %get-tuple-element.44), channel_id=1, source_target_pairs={{0,6},{1,7},{2,8},{3,9},{4,10},{5,11},{6,12},{7,13},{8,14},{9,15},... | collective-permute-start | bytes 1228808 | tf_op jit(solution)/shard_map/ppermute | solution.py:283
  17.5 45.6 %collective-permute-start.2 = (bf16[8,200,128]{2,1,0:T(8,128)(2,1)S(1)}, bf16[8,200,128]{2,1,0:T(8,128)(2,1)}, u32[]{:S(2)}, u32[]{:S(2)}) collective-permute-start(bf16[8,200,128]{2,1,0:T(8,128)(2,1)S(1)} %get-tuple-element.45), channel_id=1, source_target_pairs={{0,10},{1,11},{2,12},{3,13},{4,14},{5,15},{6,0},{7,1},{8,2},{9,3},... | collective-permute-start | bytes 1228808 | tf_op jit(solution)/shard_map/ppermute | solution.py:283
  21.0 1.7 %copy-start.1 = (bf16[2048,768]{1,0:T(8,128)(2,1)}, bf16[2048,768]{1,0:T(8,128)(2,1)S(1)}, u32[]{:S(2)}) copy-start(bf16[2048,768]{1,0:T(8,128)(2,1)S(1)} %get-tuple-element.24.emb_hbm) | copy-start | bytes 9437188 | tf_op jit(solution)/shard_map/cond
  28.2 27.4 %all-to-all-start = ((bf16[8,4,200,128]{3,2,1,0:T(8,128)(2,1)}), bf16[8,4,200,128]{3,2,1,0:T(8,128)(2,1)S(1)}, u32[]{:S(2)}, u32[]{:S(2)}) async-start(bf16[8,4,200,128]{3,2,1,0:T(8,128)(2,1)} %send_late.1), calls=%async_computation | async-start | bytes 3276800 | tf_op jit(solution)/shard_map/cond/branch_1_fun/all_to_all | solution.py:289
  56.8 34.5 %collective-permute-start.3 = (bf16[8,200,128]{2,1,0:T(8,128)(2,1)}, bf16[8,200,128]{2,1,0:T(8,128)(2,1)S(1)}, u32[]{:S(2)}, u32[]{:S(2)}) collective-permute-start(bf16[8,200,128]{2,1,0:T(8,128)(2,1)} %get-tuple-element.47), channel_id=1, source_target_pairs={{0,4},{1,5},{2,6},{3,7},{4,8},{5,9},{6,10},{7,11},{8,12},{9,13},{1... | collective-permute-start | bytes 1228808 | tf_op jit(solution)/shard_map/ppermute | solution.py:283
  58.1 33.2 %collective-permute-start.4 = (bf16[8,200,128]{2,1,0:T(8,128)(2,1)}, bf16[8,200,128]{2,1,0:T(8,128)(2,1)S(1)}, u32[]{:S(2)}, u32[]{:S(2)}) collective-permute-start(bf16[8,200,128]{2,1,0:T(8,128)(2,1)} %get-tuple-element.48), channel_id=1, source_target_pairs={{0,12},{1,13},{2,14},{3,15},{4,0},{5,1},{6,2},{7,3},{8,4},{9,5},{1... | collective-permute-start | bytes 1228808 | tf_op jit(solution)/shard_map/ppermute | solution.py:283
  60.4 30.9 %collective-permute-start.5 = (bf16[8,200,128]{2,1,0:T(8,128)(2,1)}, bf16[8,200,128]{2,1,0:T(8,128)(2,1)S(1)}, u32[]{:S(2)}, u32[]{:S(2)}) collective-permute-start(bf16[8,200,128]{2,1,0:T(8,128)(2,1)} %get-tuple-element.49), channel_id=1, source_target_pairs={{0,2},{1,3},{2,4},{3,5},{4,6},{5,7},{6,8},{7,9},{8,10},{9,11},{10,... | collective-permute-start | bytes 1228808 | tf_op jit(solution)/shard_map/ppermute | solution.py:283
  61.3 30.1 %collective-permute-start.6 = (bf16[8,200,128]{2,1,0:T(8,128)(2,1)}, bf16[8,200,128]{2,1,0:T(8,128)(2,1)S(1)}, u32[]{:S(2)}, u32[]{:S(2)}) collective-permute-start(bf16[8,200,128]{2,1,0:T(8,128)(2,1)} %get-tuple-element.50), channel_id=1, source_target_pairs={{0,14},{1,15},{2,0},{3,1},{4,2},{5,3},{6,4},{7,5},{8,6},{9,7},{10,... | collective-permute-start | bytes 1228808 | tf_op jit(solution)/shard_map/ppermute | solution.py:283

commit v3 on v2

--- a/solution.py
+++ b/solution.py
@@ -83,28 +83,27 @@
     return goal
 
 
-def unit_rows(goal, first, size, emb):
-    pick = (iota((size, emb.shape[0]), 0) + first == goal).astype(BF16)
-    moved = dot(pick, emb)
+def scaled(moved):
     inverse = lax.rsqrt(jnp.sum(moved * moved, axis=1, keepdims=True) + 1e-06)
     return (moved * inverse).astype(BF16)
 
 
-def pack(unit, meta, per_pair):
-    blocks = unit.shape[0] // per_pair
-    parts = [
-        unit[:, c * LANES : (c + 1) * LANES].reshape(blocks, per_pair, LANES)
-        for c in range(unit.shape[1] // LANES)
-    ]
-    parts.append(jnp.broadcast_to(meta[:, None, :], (blocks, META, LANES)).astype(BF16))
-    return parts
-
-
-def put_parts(ref, parts):
-    at = 0
-    for part in parts:
-        ref[..., at : at + part.shape[-2], :] = part
-        at += part.shape[-2]
+def picked(goal, first, size):
+    return (iota((size, goal.shape[1]), 0) + first == goal).astype(BF16)
+
+
+def put_pair(ref, at, unit):
+    rows = unit.shape[0]
+    for c in range(unit.shape[1] // LANES):
+        ref[at + c * rows : at + (c + 1) * rows, :] = unit[:, c * LANES : (c + 1) * LANES]
+
+
+def put_block(ref, unit, meta):
+    rows = unit.shape[0] // PLANE
+    tall = ref.shape[0] // PLANE - 1
+    for p in range(PLANE):
+        put_pair(ref, p * tall, unit[p * rows : (p + 1) * rows])
+    ref[PLANE * tall :, :] = meta.astype(BF16)
 
 
 def first_kernel(
@@ -123,44 +122,54 @@
     put_row(pos_ref, pos)
     meta_ref[...] = meta
     flag_ref[0] = 1
+    pick = picked(place(pos, per_pair, EARLY[:1], False), 0, PLANE * per_pair)
     copies[2].wait()
-    unit = unit_rows(place(pos, per_pair, EARLY[:1], False), 0, PLANE * per_pair, emb_ref[...])
     shift = EARLY[0]
-    put_parts(out_ref, pack(unit, meta[shift * PLANE : (shift + 1) * PLANE], per_pair))
-
-
-def some_kernel(per_pair, shifts, pos_ref, meta_ref, emb_hbm, *refs):
-    *outs, emb_ref, sem = refs
-    copy = pltpu.make_async_copy(emb_hbm, emb_ref, sem)
-    copy.start()
+    put_block(out_ref, scaled(dot(pick, emb_ref[...])), meta[shift * PLANE : (shift + 1) * PLANE])
+
+
+def some_kernel(per_pair, shifts, pos_ref, meta_ref, emb_ref, *outs):
+    size = PLANE * per_pair
     goal = place(wide_row(pos_ref), per_pair, shifts, False)
-    copy.wait()
-    size = PLANE * per_pair
-    unit = unit_rows(goal, 0, size * len(outs), emb_ref[...])
+    unit = scaled(dot(picked(goal, 0, size * len(outs)), emb_ref[...]))
     for k, (shift, out_ref) in enumerate(zip(shifts, outs)):
-        meta = meta_ref[shift * PLANE : (shift + 1) * PLANE, :]
-        put_parts(out_ref, pack(unit[k * size : (k + 1) * size], meta, per_pair))
-
-
-def late_kernel(per_pair, pos_ref, meta_ref, emb_hbm, out_ref, emb_ref, goal_scr, sem):
-    step = pl.program_id(0)
-    per_step = out_ref.shape[0]
-    size = per_step * len(LATE) * per_pair
-
-    @pl.when(step == 0)
-    def _():
-        copy = pltpu.make_async_copy(emb_hbm, emb_ref, sem)
-        copy.start()
-        goal_scr[...] = place(wide_row(pos_ref), per_pair, LATE, True)
-        copy.wait()
-
-    unit = unit_rows(goal_scr[...], step * size, size, emb_ref[...])
-    for p in range(per_step):
-        for k, shift in enumerate(LATE):
-            at = (p * len(LATE) + k) * per_pair
-            meta = meta_ref[pl.ds(shift * PLANE + step * per_step + p, 1), :]
-            parts = pack(unit[at : at + per_pair], meta, per_pair)
-            put_parts(out_ref.at[p, k], [part[0] for part in parts])
+        put_block(out_ref, unit[k * size : (k + 1) * size], meta_ref[shift * PLANE : (shift + 1) * PLANE, :])
+
+
+def late_kernel(per_pair, _, pos_ref, meta_ref, emb_ref, late_ref):
+    goal = place(wide_row(pos_ref), per_pair, LATE, True)
+    some = len(LATE) * per_pair
+    tall = emb_ref.shape[1] // LANES * per_pair
+    step = 512 // some
+    for p0 in range(0, PLANE, step):
+        unit = scaled(dot(picked(goal, p0 * some, step * some), emb_ref[...]))
+        for p in range(p0, p0 + step):
+            for k in range(len(LATE)):
+                at = ((p - p0) * len(LATE) + k) * per_pair
+                put_pair(late_ref.at[p], k * tall, unit[at : at + per_pair])
+            meta = [meta_ref[shift * PLANE + p : shift * PLANE + p + 1, :] for shift in LATE]
+            meta.append(jnp.zeros((META - len(LATE), LANES), F32))
+            late_ref[p, len(LATE) * tall :, :] = jnp.concatenate(meta, axis=0).astype(BF16)
+
+
+def cut_kernel(got_ref, *outs):
+    tall = outs[0].shape[0] // PLANE - 1
+    meta = got_ref[:, len(outs) * tall :, :].astype(F32)
+    for k, out_ref in enumerate(outs):
+        for p in range(PLANE):
+            out_ref[p * tall : (p + 1) * tall, :] = got_ref[p, k * tall : (k + 1) * tall, :]
+        out_ref[PLANE * tall :, :] = meta[:, k, :].astype(BF16)
+
+
+def merge_kernel(*refs):
+    *ins, out_ref = refs
+    tall = ins[0].shape[0] // PLANE - 1
+    metas = [ref[PLANE * tall :, :].astype(F32) for ref in ins]
+    for p in range(PLANE):
+        for k, ref in enumerate(ins):
+            out_ref[p, k * tall : (k + 1) * tall, :] = ref[p * tall : (p + 1) * tall, :]
+        meta = [m[p : p + 1, :] for m in metas] + [jnp.zeros((META - len(ins), LANES), F32)]
+        out_ref[p, len(ins) * tall :, :] = jnp.concatenate(meta, axis=0).astype(BF16)
 
 
 def piece_weights(lane, per_pair):
@@ -170,25 +179,32 @@
 
 
 def best_kernel(per_pair, early_ref, *refs):
-    *late, out_ref, col_scr, base_scr, row_scr, across_scr = refs
+    *late, out_ref, col_scr, group_scr, row_scr, across_scr = refs
     rows = col_scr.shape[0]
-    blocks = [early_ref.at[:, k] for k in range(len(EARLY))] + list(late)
-    chunks = early_ref.shape[2] // per_pair
+    tall = late[0].shape[0] // PLANE - 1
+    chunks = tall // per_pair
     span = float(1 << INDEX_BITS)
 
+    def pairs(t, at):
+        if t < len(EARLY):
+            return early_ref[:, t * tall + at : t * tall + at + per_pair, :].reshape(TILE, LANES)
+        ref = late[t - len(EARLY)]
+        return jnp.concatenate(
+            [ref[p * tall + at : p * tall + at + per_pair, :] for p in range(PLANE)], axis=0
+        )
+
     def tile(t):
-        return jnp.concatenate(
-            [blocks[t][:, c * per_pair : (c + 1) * per_pair, :].reshape(TILE, LANES) for c in range(chunks)], axis=1
-        )
-
-    meta = [block[:, chunks * per_pair :, :].astype(F32)[:, 0:1, :] for block in blocks]
-    meta = jnp.concatenate(meta, axis=0)
+        return jnp.concatenate([pairs(t, c * per_pair) for c in range(chunks)], axis=1)
+
+    meta = early_ref[:, len(EARLY) * tall :, :].astype(F32)
+    meta = [meta[:, k, :] for k in range(len(EARLY))] + [ref[PLANE * tall :, :].astype(F32) for ref in late]
+    meta = jnp.concatenate(meta, axis=0)[:, None, :]
     meta = jnp.broadcast_to(meta, (rows // per_pair, per_pair, LANES)).reshape(rows, LANES)
     own = (iota((rows, LANES), 0) % per_pair) == (iota((rows, LANES), 1) % per_pair)
     meta = jnp.where(own, meta, 0.0).astype(BF16)
     col = dot(meta, piece_weights(iota((LANES, LANES), 0), per_pair))
     col_scr[...] = col
-    base_scr[...] = jnp.floor(col * (1.0 / span)) * span
+    group_scr[...] = jnp.floor(col * (1.0 / span))
     row_scr[...] = dot_t(piece_weights(iota((8, LANES), 1), per_pair), meta)
     across_scr[...] = jnp.full(across_scr.shape, -1.0, F32)
 
@@ -196,19 +212,19 @@
     for i in range(rows // TILE):
         mine = tile(i)
         row = [row_scr[0:1, i * TILE + b : i * TILE + b + LANES] for b in range(0, TILE, LANES)]
-        base = [jnp.floor(r * (1.0 / span)) * span for r in row]
+        group = [jnp.floor(r * (1.0 / span)) for r in row]
         best = [jnp.full((1, LANES), -1.0, F32) for _ in row]
         for j in range(i + 1):
             at = slice(j * TILE, (j + 1) * TILE)
             scores = dot_t(tile(j), mine)
-            col, low = col_scr[at, :], base_scr[at, :]
+            col, col_group = col_scr[at, :], group_scr[at, :]
             across = across_scr[at, :]
             for b in range(len(row)):
-                part = scores[:, b * LANES : (b + 1) * LANES]
-                kept = jnp.where((col < row[b]) & (col >= base[b]), part, -1.0)
-                best[b] = jnp.maximum(best[b], jnp.max(kept, axis=0, keepdims=True))
+                part = jnp.where(col_group == group[b], scores[:, b * LANES : (b + 1) * LANES], -1.0)
+                before = col < row[b]
+                best[b] = jnp.maximum(best[b], jnp.max(jnp.where(before, part, -1.0), axis=0, keepdims=True))
                 if j < i:
-                    across = jnp.maximum(across, jnp.where((row[b] < col) & (row[b] >= low), part, -1.0))
+                    across = jnp.maximum(across, jnp.where(before, -1.0, part))
             if j < i:
                 across_scr[at, :] = across
         down += best
@@ -262,6 +278,7 @@
 
 
 ANY = pl.BlockSpec(memory_space=pl.ANY)
+VMEM = pl.BlockSpec(memory_space=pltpu.VMEM)
 FIRST = pltpu.CompilerParams(vmem_limit_bytes=61 * 1024 * 1024)
 LIMIT = pltpu.CompilerParams(vmem_limit_bytes=24 * 1024 * 1024)
 
@@ -301,8 +318,8 @@
     per_owner = CLUSTERS // members
     per_pair = rows // members
     lines = rows // LANES
-    tall = width // LANES * per_pair + META
-    block = (PLANE, tall, LANES)
+    tall = width // LANES * per_pair
+    block = (PLANE * (tall + 1), LANES)
     one, pos, meta, flag = pl.pallas_call(
         functools.partial(first_kernel, members, per_owner, per_pair),
         in_specs=[ANY, ANY, ANY],
@@ -325,45 +342,40 @@
     )(cluster_id.reshape(lines, LANES), row_index.reshape(lines, LANES), embeds)
     got = [to_shift(one, EARLY[0])]
 
-    def send_some(shifts, name, pos, meta, embeds):
+    def send(kernel, shifts, more, name):
         return pl.pallas_call(
-            functools.partial(some_kernel, per_pair, shifts),
-            in_specs=[whole((lines, LANES)), whole((members, LANES)), ANY],
-            out_shape=[shape(block, BF16) for _ in shifts],
-            scratch_shapes=[pltpu.VMEM((rows, width), BF16), pltpu.SemaphoreType.DMA],
+            functools.partial(kernel, per_pair, shifts),
+            in_specs=[whole((lines, LANES)), whole((members, LANES)), VMEM],
+            out_shape=[shape(block, BF16) for _ in shifts] + more,
             compiler_params=LIMIT,
             cost_estimate=cost(len(shifts) * TILE * rows * width),
             name=name,
-        )(pos, meta, embeds)
-
-    more = send_some(EARLY[1:-1], "send_early", pos, meta, embeds)
-    got += [to_shift(x, dz) for x, dz in zip(more, EARLY[1:-1])]
+        )
+
+    more = send(some_kernel, EARLY[1:3], [], "send_early")(pos, meta, embeds)
+    got += [to_shift(x, dz) for x, dz in zip(more, EARLY[1:3])]
 
     def late_part(pos, meta, embeds):
-        steps = 4
-        late = pl.pallas_call(
-            functools.partial(late_kernel, per_pair),
-            grid=(steps,),
-            in_specs=[whole((lines, LANES)), whole((members, LANES)), ANY],
-            out_specs=pl.BlockSpec((PLANE // steps, len(LATE), tall, LANES), lambda s: (s, 0, 0, 0)),
-            out_shape=shape((PLANE, len(LATE), tall, LANES), BF16),
-            scratch_shapes=[
-                pltpu.VMEM((rows, width), BF16),
-                pltpu.VMEM((1, rows), I32),
-                pltpu.SemaphoreType.DMA,
-            ],
-            compiler_params=LIMIT,
-            cost_estimate=cost(len(LATE) * TILE * rows * width),
-            name="send_late",
-        )(pos, meta, embeds)
-        late = in_plane(late)
-        return [late[:, k] for k in range(len(LATE))] + list(
-            send_some(EARLY[-1:], "send_own", pos, meta, embeds)
-        )
+        late = send(late_kernel, (), [shape((PLANE, len(LATE) * tall + META, LANES), BF16)], "send_late")
+        late = in_plane(late(pos, meta, embeds)[0])
+        parts = pl.pallas_call(
+            cut_kernel, out_shape=[shape(block, BF16) for _ in LATE], compiler_params=LIMIT, name="cut"
+        )(late)
+        return parts + send(some_kernel, (0,), [], "send_own")(pos, meta, embeds)
 
     *moving, own = step_of_its_own(late_part, flag, pos, meta, embeds)
     shifted = [to_shift(x, dz) for x, dz in zip(moving, LATE)]
-    early = step_of_its_own(lambda *got: in_plane(jnp.stack(got, axis=1)), flag, *got, own)
+
+    def last_part(got):
+        early = pl.pallas_call(
+            merge_kernel,
+            out_shape=shape((PLANE, len(got) * tall + META, LANES), BF16),
+            compiler_params=LIMIT,
+            name="merge",
+        )(*got)
+        return in_plane(early)
+
+    early = step_of_its_own(last_part, flag, got + [own])
     best = pl.pallas_call(
         functools.partial(best_kernel, per_pair),
         out_shape=shape((members, per_pair), F32),

time: 114 us -> 109 us (0.956)
  local copies, waits for them, and re-layouts: 2.85 us -> 0 us
  other arithmetic: 1.33 us -> 0 us
  blocking collectives: 40.3 us -> 39 us
    pallas_call x3 -> x5, Pallas kernels: 12.5 us -> 16 us  [the longest x1 6.63 us: late_part(): late = in_plane(late(pos, meta, embeds)[0])]
    pallas_call x1, Pallas kernels: 8.28 us -> 5.55 us  [on_device(): pl.pallas_call(functools.partial(best_kernel, per_pair), out_shape=shape(...]
    cond x2 -> x0, local copies, waits for them, and re-layouts: 1.64 us -> none
    another operation x1 -> x0, other arithmetic: 1.33 us -> none  [on_device(): jnp.stack(got, axis=1)]
    squeeze x1 -> x0, local copies, waits for them, and re-layouts: 1.2 us -> none  [late_part(): late[:, k]]
  transfers between devices with their start and end apart: 8 -> 8, of which waited for: 1 -> 1; matrix products, arithmetic and copies ran while one was open for 2% -> 0% of each run, Pallas kernels for 11% -> 15%
where the time goes in v3:
time: 109 us
  blocking collectives  39 us (36%)
  Pallas kernels  26.5 us (24%)
  starting transfers between devices  24.6 us (23%)
  waiting for transfers between devices  17.8 us (16%)
    all_to_all x1, blocking collectives, in_plane(): lax.all_to_all(rows, 'member', split_axis=0, concat_axis=0, tiled=True, a...  25.9 us
    ppermute x7, starting transfers between devices, to_shift(): return lax.ppermute(rows, 'member', pairs)  18.6 us
    all_to_all x1, waiting for transfers between devices, in_plane(): lax.all_to_all(rows, 'member', split_axis=0, concat_axis=0, tiled=True, a...  17.8 us
    all_to_all x1, blocking collectives, on_device(): lax.all_to_all(best, 'member', split_axis=0, concat_axis=0, tiled=True)  13.1 us
    pallas_call x1, Pallas kernels, late_part(): late = in_plane(late(pos, meta, embeds)[0])  6.63 us
    all_to_all x1, starting transfers between devices, in_plane(): lax.all_to_all(rows, 'member', split_axis=0, concat_axis=0, tiled=True, a...  5.99 us
    pallas_call x1, Pallas kernels, on_device(): pl.pallas_call(functools.partial(best_kernel, per_pair), out_shape=shape(...  5.55 us
    pallas_call x1, Pallas kernels, on_device(): pl.pallas_call(functools.partial(first_kernel, members, per_owner, per_pa...  3.92 us
  transfers between devices with their start and end apart: 8, of which 1 were waited for; matrix products, arithmetic and copies ran while one was open for 0% of the time, Pallas kernels for 15%

profile of v3, /device:TPU:1, one launch (start us, length us, event | category | flops | bytes accessed | tf_op | source)
XLA Modules:
  0.0 108.7 jit_solution(7086722266110573521)
XLA Ops:
  0.0 3.9 %send_first.1 = (bf16[1544,128]{1,0:T(8,128)(2,1)}, s32[16,128]{1,0:T(8,128)S(1)}, f32[64,128]{1,0:T(8,128)S(1)}, s32[1]{0:T(128)}) custom-call(s32[16,128]{1,0:T(8,128)} %bitcast.10, s32[16,128]{1,0:T(8,128)} %bitcast.11, bf16[2048,768]{1,0:T(8,128)(2,1)} %emb_ref.1), custom_call_target="tpu_custom_call" | custom-call | flops 805306368 | bytes 8388608 | tf_op jit(solution)/shard_map/send_first/pallas_call | solution.py:323
  3.9 7.8 %collective-permute-start = (bf16[1544,128]{1,0:T(8,128)(2,1)}, bf16[1544,128]{1,0:T(8,128)(2,1)S(1)}, u32[]{:S(2)}, u32[]{:S(2)}) collective-permute-start(bf16[1544,128]{1,0:T(8,128)(2,1)} %get-tuple-element.45), channel_id=1, source_target_pairs={{0,8},{1,9},{2,10},{3,11},{4,12},{5,13},{6,14},{7,15},{8,0},{9,1},... | collective-permute-start | bytes 1185800 | tf_op jit(solution)/shard_map/ppermute | solution.py:300
  11.8 3.9 %send_early.1 = (bf16[1544,128]{1,0:T(8,128)(2,1)S(1)}, bf16[1544,128]{1,0:T(8,128)(2,1)S(1)}) custom-call(s32[16,128]{1,0:T(8,128)S(1)} %get-tuple-element.46.pos_ref, f32[64,128]{1,0:T(8,128)S(1)} %get-tuple-element.47.meta_ref, bf16[2048,768]{1,0:T(8,128)(2,1)} %emb_ref.1), custom_call_target="tpu_custom_call" | custom-call | flops 1610612736 | bytes 8388608 | tf_op jit(solution)/shard_map/send_early/pallas_call | solution.py:355
  15.6 1.7 %collective-permute-start.1 = (bf16[1544,128]{1,0:T(8,128)(2,1)S(1)}, bf16[1544,128]{1,0:T(8,128)(2,1)}, u32[]{:S(2)}, u32[]{:S(2)}) collective-permute-start(bf16[1544,128]{1,0:T(8,128)(2,1)S(1)} %get-tuple-element.48), channel_id=1, source_target_pairs={{0,6},{1,7},{2,8},{3,9},{4,10},{5,11},{6,12},{7,13},{8,14},{9,15},... | collective-permute-start | bytes 1185800 | tf_op jit(solution)/shard_map/ppermute | solution.py:300
  17.4 2.8 %collective-permute-start.2 = (bf16[1544,128]{1,0:T(8,128)(2,1)S(1)}, bf16[1544,128]{1,0:T(8,128)(2,1)}, u32[]{:S(2)}, u32[]{:S(2)}) collective-permute-start(bf16[1544,128]{1,0:T(8,128)(2,1)S(1)} %get-tuple-element.49), channel_id=1, source_target_pairs={{0,10},{1,11},{2,12},{3,13},{4,14},{5,15},{6,0},{7,1},{8,2},{9,3},... | collective-permute-start | bytes 1185800 | tf_op jit(solution)/shard_map/ppermute | solution.py:300
  20.8 34.8 %conditional.2 = (bf16[1544,128]{1,0:T(8,128)(2,1)}, bf16[1544,128]{1,0:T(8,128)(2,1)}, bf16[1544,128]{1,0:T(8,128)(2,1)}, bf16[1544,128]{1,0:T(8,128)(2,1)}, bf16[1544,128]{1,0:T(8,128)(2,1)S(1)}) conditional(s32[]{:T(128)} %bitcast.2, () %tuple.20, (s32[16,128]{1,0:T(8,128)S(1)}, f32[64,128]{1,0:T(8,128)S(1)}, bf16[2048,768]{1,0:T(8,128)(2,1)}) %tuple.21), branch_computations={%region_0.0_spmd, %region_1.0_spmd} | conditional | flops 805306368 | bytes 21545032 | solution.py:312
  20.9 6.6 %send_late.1 = bf16[8,776,128]{2,1,0:T(8,128)(2,1)} custom-call(s32[16,128]{1,0:T(8,128)S(1)} %get-tuple-element.22.pos_ref, f32[64,128]{1,0:T(8,128)S(1)} %get-tuple-element.23.meta_ref, bf16[2048,768]{1,0:T(8,128)(2,1)} %get-tuple-element.24.emb_ref), custom_call_target="tpu_custom_call" | custom-call | bytes 8388608 | tf_op jit(solution)/shard_map/cond/branch_1_fun/send_late/pallas_call | solution.py:360
  27.5 6.0 %all-to-all-start = ((bf16[8,776,128]{2,1,0:T(8,128)(2,1)}), bf16[8,776,128]{2,1,0:T(8,128)(2,1)S(1)}, u32[]{:S(2)}, u32[]{:S(2)}) async-start(bf16[8,776,128]{2,1,0:T(8,128)(2,1)} %send_late.1), calls=%async_computation | async-start | bytes 3178496 | tf_op jit(solution)/shard_map/cond/branch_1_fun/all_to_all | solution.py:306
  33.5 3.1 %send_own.1 = bf16[1544,128]{1,0:T(8,128)(2,1)S(1)} custom-call(s32[16,128]{1,0:T(8,128)S(1)} %get-tuple-element.22.pos_ref, f32[64,128]{1,0:T(8,128)S(1)} %get-tuple-element.23.meta_ref, bf16[2048,768]{1,0:T(8,128)(2,1)} %get-tuple-element.24.emb_ref), custom_call_target="tpu_custom_call" | custom-call | flops 805306368 | bytes 8388608 | tf_op jit(solution)/shard_map/cond/branch_1_fun/send_own/pallas_call | solution.py:364
  36.5 17.8 %all-to-all-done.got_ref = bf16[8,776,128]{2,1,0:T(8,128)(2,1)S(1)} async-done(((bf16[8,776,128]{2,1,0:T(8,128)(2,1)}), bf16[8,776,128]{2,1,0:T(8,128)(2,1)S(1)}, u32[]{:S(2)}, u32[]{:S(2)}) %all-to-all-start) | async-done | bytes 1589280 | tf_op jit(solution)/shard_map/cond/branch_1_fun/all_to_all | solution.py:306
  54.4 1.2 %cut.1 = (bf16[1544,128]{1,0:T(8,128)(2,1)}, bf16[1544,128]{1,0:T(8,128)(2,1)}, bf16[1544,128]{1,0:T(8,128)(2,1)}, bf16[1544,128]{1,0:T(8,128)(2,1)}) custom-call(bf16[8,776,128]{2,1,0:T(8,128)(2,1)S(1)} %all-to-all-done.got_ref), custom_call_target="tpu_custom_call" | custom-call | tf_op jit(solution)/shard_map/cond/branch_1_fun/cut/pallas_call | solution.py:361
  55.6 1.3 %collective-permute-start.3 = (bf16[1544,128]{1,0:T(8,128)(2,1)}, bf16[1544,128]{1,0:T(8,128)(2,1)S(1)}, u32[]{:S(2)}, u32[]{:S(2)}) collective-permute-start(bf16[1544,128]{1,0:T(8,128)(2,1)} %get-tuple-element.51), channel_id=1, source_target_pairs={{0,4},{1,5},{2,6},{3,7},{4,8},{5,9},{6,10},{7,11},{8,12},{9,13},{1... | collective-permute-start | bytes 1185800 | tf_op jit(solution)/shard_map/ppermute | solution.py:300
  56.9 2.3 %collective-permute-start.4 = (bf16[1544,128]{1,0:T(8,128)(2,1)}, bf16[1544,128]{1,0:T(8,128)(2,1)S(1)}, u32[]{:S(2)}, u32[]{:S(2)}) collective-permute-start(bf16[1544,128]{1,0:T(8,128)(2,1)} %get-tuple-element.52), channel_id=1, source_target_pairs={{0,12},{1,13},{2,14},{3,15},{4,0},{5,1},{6,2},{7,3},{8,4},{9,5},{1... | collective-permute-start | bytes 1185800 | tf_op jit(solution)/shard_map/ppermute | solution.py:300
  59.2 0.0 collective-permute-done
  59.2 0.9 collective-permute-start.5
  60.0 1.8 %collective-permute-start.6 = (bf16[1544,128]{1,0:T(8,128)(2,1)}, bf16[1544,128]{1,0:T(8,128)(2,1)S(1)}, u32[]{:S(2)}, u32[]{:S(2)}) collective-permute-start(bf16[1544,128]{1,0:T(8,128)(2,1)} %get-tuple-element.54), channel_id=1, source_target_pairs={{0,14},{1,15},{2,0},{3,1},{4,2},{5,3},{6,4},{7,5},{8,6},{9,7},{10,... | collective-permute-start | bytes 1185800 | tf_op jit(solution)/shard_map/ppermute | solution.py:300
  61.9 0.0 collective-permute-done.2
  61.9 27.1 %conditional.3 = (bf16[8,776,128]{2,1,0:T(8,128)(2,1)S(1)}) conditional(s32[]{:T(128)} %bitcast.2, () %tuple.19, (bf16[1544,128]{1,0:T(8,128)(2,1)S(1)}, bf16[1544,128]{1,0:T(8,128)(2,1)}, bf16[1544,128]{1,0:T(8,128)(2,1)}, bf16[1544,128]{1,0:T(8,128)(2,1)S(1)}) %tuple.22), branch_computations={%region_2.0_spmd, %region_3.0_spmd} | conditional | bytes 3178504 | solution.py:312
  61.9 1.2 %merge.1 = bf16[8,776,128]{2,1,0:T(8,128)(2,1)S(1)} custom-call(bf16[1544,128]{1,0:T(8,128)(2,1)S(1)} %get-tuple-element.29.refs_0_, bf16[1544,128]{1,0:T(8,128)(2,1)} %get-tuple-element.30.refs_1_, bf16[1544,128]{1,0:T(8,128)(2,1)} %get-tuple-element.31.refs_2_, bf16[1544,128]{1,0:T(8,128)(2,1)S(1)} %get-tuple-element.32.refs_3_), custom_call_target="tpu_custom_call" | custom-call | tf_op jit(solution)/shard_map/cond/branch_1_fun/merge/pallas_call | solution.py:370
  63.1 25.9 %all_to_all.19 = bf16[8,776,128]{2,1,0:T(8,128)(2,1)S(1)} all-to-all(bf16[8,776,128]{2,1,0:T(8,128)(2,1)S(1)} %merge.1), channel_id=1, replica_groups={{0,1,16,17,32,33,48,49},{2,3,18,19,34,35,50,51},{4,5,20,21,36,37,52,53}..., dimensions={0} | all-to-all | bytes 3178496 | tf_op jit(solution)/shard_map/cond/branch_1_fun/all_to_all | solution.py:306
  89.0 0.0 collective-permute-done.3.refs_0_
  89.0 5.6 %best.1 = f32[64,32]{1,0:T(8,128)S(1)} custom-call(bf16[8,776,128]{2,1,0:T(8,128)(2,1)S(1)} %get-tuple-element.65.early_ref, bf16[1544,128]{1,0:T(8,128)(2,1)S(1)} %collective-permute-done.3.refs_0_, bf16[1544,128]{1,0:T(8,128)(2,1)S(1)} %collective-permute-done.4.refs_1_, bf16[1544,128]{1,0:T(8,128)(2,1)S(1)} %collective-permute-done.5.refs_2_, ...), custom_call_target="tpu_custom_call" | custom-call | flops 3221225472 | bytes 8388608 | tf_op jit(solution)/shard_map/best/pallas_call | solution.py:379
  94.6 13.1 %all_to_all.20 = f32[64,1,32]{2,1,0:T(1,128)S(1)} all-to-all(f32[64,1,32]{2,1,0:T(1,128)S(1)} %bitcast.9), channel_id=1, replica_groups=mesh['outer'=4,'member'=64] {'member'}, dimensions={0} | all-to-all | bytes 16384 | tf_op jit(solution)/shard_map/all_to_all | solution.py:392
  107.7 1.0 home.1
  (4 shorter events, 0.0 us)
Async XLA Ops:
  3.9 55.2 %collective-permute-start = (bf16[1544,128]{1,0:T(8,128)(2,1)}, bf16[1544,128]{1,0:T(8,128)(2,1)S(1)}, u32[]{:S(2)}, u32[]{:S(2)}) collective-permute-start(bf16[1544,128]{1,0:T(8,128)(2,1)} %get-tuple-element.45), channel_id=1, source_target_pairs={{0,8},{1,9},{2,10},{3,11},{4,12},{5,13},{6,14},{7,15},{8,0},{9,1},... | collective-permute-start | bytes 1185800 | tf_op jit(solution)/shard_map/ppermute | solution.py:300
  15.6 44.4 %collective-permute-start.1 = (bf16[1544,128]{1,0:T(8,128)(2,1)S(1)}, bf16[1544,128]{1,0:T(8,128)(2,1)}, u32[]{:S(2)}, u32[]{:S(2)}) collective-permute-start(bf16[1544,128]{1,0:T(8,128)(2,1)S(1)} %get-tuple-element.48), channel_id=1, source_target_pairs={{0,6},{1,7},{2,8},{3,9},{4,10},{5,11},{6,12},{7,13},{8,14},{9,15},... | collective-permute-start | bytes 1185800 | tf_op jit(solution)/shard_map/ppermute | solution.py:300
  17.4 44.5 %collective-permute-start.2 = (bf16[1544,128]{1,0:T(8,128)(2,1)S(1)}, bf16[1544,128]{1,0:T(8,128)(2,1)}, u32[]{:S(2)}, u32[]{:S(2)}) collective-permute-start(bf16[1544,128]{1,0:T(8,128)(2,1)S(1)} %get-tuple-element.49), channel_id=1, source_target_pairs={{0,10},{1,11},{2,12},{3,13},{4,14},{5,15},{6,0},{7,1},{8,2},{9,3},... | collective-permute-start | bytes 1185800 | tf_op jit(solution)/shard_map/ppermute | solution.py:300
  27.5 26.9 %all-to-all-start = ((bf16[8,776,128]{2,1,0:T(8,128)(2,1)}), bf16[8,776,128]{2,1,0:T(8,128)(2,1)S(1)}, u32[]{:S(2)}, u32[]{:S(2)}) async-start(bf16[8,776,128]{2,1,0:T(8,128)(2,1)} %send_late.1), calls=%async_computation | async-start | bytes 3178496 | tf_op jit(solution)/shard_map/cond/branch_1_fun/all_to_all | solution.py:306
  55.6 33.4 %collective-permute-start.3 = (bf16[1544,128]{1,0:T(8,128)(2,1)}, bf16[1544,128]{1,0:T(8,128)(2,1)S(1)}, u32[]{:S(2)}, u32[]{:S(2)}) collective-permute-start(bf16[1544,128]{1,0:T(8,128)(2,1)} %get-tuple-element.51), channel_id=1, source_target_pairs={{0,4},{1,5},{2,6},{3,7},{4,8},{5,9},{6,10},{7,11},{8,12},{9,13},{1... | collective-permute-start | bytes 1185800 | tf_op jit(solution)/shard_map/ppermute | solution.py:300
  56.9 32.1 %collective-permute-start.4 = (bf16[1544,128]{1,0:T(8,128)(2,1)}, bf16[1544,128]{1,0:T(8,128)(2,1)S(1)}, u32[]{:S(2)}, u32[]{:S(2)}) collective-permute-start(bf16[1544,128]{1,0:T(8,128)(2,1)} %get-tuple-element.52), channel_id=1, source_target_pairs={{0,12},{1,13},{2,14},{3,15},{4,0},{5,1},{6,2},{7,3},{8,4},{9,5},{1... | collective-permute-start | bytes 1185800 | tf_op jit(solution)/shard_map/ppermute | solution.py:300
  59.2 29.8 %collective-permute-start.5 = (bf16[1544,128]{1,0:T(8,128)(2,1)}, bf16[1544,128]{1,0:T(8,128)(2,1)S(1)}, u32[]{:S(2)}, u32[]{:S(2)}) collective-permute-start(bf16[1544,128]{1,0:T(8,128)(2,1)} %get-tuple-element.53), channel_id=1, source_target_pairs={{0,2},{1,3},{2,4},{3,5},{4,6},{5,7},{6,8},{7,9},{8,10},{9,11},{10,... | collective-permute-start | bytes 1185800 | tf_op jit(solution)/shard_map/ppermute | solution.py:300
  60.0 29.0 %collective-permute-start.6 = (bf16[1544,128]{1,0:T(8,128)(2,1)}, bf16[1544,128]{1,0:T(8,128)(2,1)S(1)}, u32[]{:S(2)}, u32[]{:S(2)}) collective-permute-start(bf16[1544,128]{1,0:T(8,128)(2,1)} %get-tuple-element.54), channel_id=1, source_target_pairs={{0,14},{1,15},{2,0},{3,1},{4,2},{5,3},{6,4},{7,5},{8,6},{9,7},{10,... | collective-permute-start | bytes 1185800 | tf_op jit(solution)/shard_map/ppermute | solution.py:300

commit v4 on v3

--- a/solution.py
+++ b/solution.py
@@ -15,7 +15,8 @@
 NZ, CORES, PLANE = 8, 2, 8
 EARLY = (4, 3, 5, 0)
 LATE = (2, 6, 1, 7)
-ORDER = EARLY + LATE
+SOON, NEXT = (4,), (3, 5, 0)
+ORDER = LATE + EARLY
 BF16, F32, I32 = jnp.bfloat16, jnp.float32, jnp.int32
 
 
@@ -106,10 +107,15 @@
     ref[PLANE * tall :, :] = meta.astype(BF16)
 
 
-def first_kernel(
-    owners, per_owner, per_pair, cid_hbm, idx_hbm, emb_hbm, out_ref, pos_ref, meta_ref, flag_ref,
-    cid_ref, idx_ref, emb_ref, sem
-):
+def put_blocks(outs, shifts, goal, meta_ref, emb_ref, per_pair):
+    size = PLANE * per_pair
+    unit = scaled(dot(picked(goal, 0, size * len(outs)), emb_ref[...]))
+    for k, (shift, out_ref) in enumerate(zip(shifts, outs)):
+        put_block(out_ref, unit[k * size : (k + 1) * size], meta_ref[shift * PLANE : (shift + 1) * PLANE, :])
+
+
+def first_kernel(owners, per_owner, per_pair, cid_hbm, idx_hbm, emb_hbm, *refs):
+    *outs, pos_ref, meta_ref, flag_ref, emb_ref, cid_ref, idx_ref, sem = refs
     copies = [
         pltpu.make_async_copy(src, dst, sem.at[n])
         for n, (src, dst) in enumerate(((cid_hbm, cid_ref), (idx_hbm, idx_ref), (emb_hbm, emb_ref)))
@@ -122,21 +128,19 @@
     put_row(pos_ref, pos)
     meta_ref[...] = meta
     flag_ref[0] = 1
-    pick = picked(place(pos, per_pair, EARLY[:1], False), 0, PLANE * per_pair)
+    goal = place(pos, per_pair, SOON, False)
     copies[2].wait()
-    shift = EARLY[0]
-    put_block(out_ref, scaled(dot(pick, emb_ref[...])), meta[shift * PLANE : (shift + 1) * PLANE])
+    put_blocks(outs, SOON, goal, meta_ref, emb_ref, per_pair)
 
 
 def some_kernel(per_pair, shifts, pos_ref, meta_ref, emb_ref, *outs):
-    size = PLANE * per_pair
     goal = place(wide_row(pos_ref), per_pair, shifts, False)
-    unit = scaled(dot(picked(goal, 0, size * len(outs)), emb_ref[...]))
-    for k, (shift, out_ref) in enumerate(zip(shifts, outs)):
-        put_block(out_ref, unit[k * size : (k + 1) * size], meta_ref[shift * PLANE : (shift + 1) * PLANE, :])
-
-
-def late_kernel(per_pair, _, pos_ref, meta_ref, emb_ref, late_ref):
+    put_blocks(outs, shifts, goal, meta_ref, emb_ref, per_pair)
+
+
+def rest_kernel(per_pair, shifts, pos_ref, meta_ref, emb_ref, *refs):
+    *outs, late_ref = refs
+    some_kernel(per_pair, shifts, pos_ref, meta_ref, emb_ref, *outs)
     goal = place(wide_row(pos_ref), per_pair, LATE, True)
     some = len(LATE) * per_pair
     tall = emb_ref.shape[1] // LANES * per_pair
@@ -178,38 +182,46 @@
     return value.astype(BF16)
 
 
-def best_kernel(per_pair, early_ref, *refs):
-    *late, out_ref, col_scr, group_scr, row_scr, across_scr = refs
+def best_kernel(per_pair, early_hbm, *refs):
+    *late, out_ref, early_ref, col_scr, group_scr, row_scr, across_scr, sem = refs
+    copy = pltpu.make_async_copy(early_hbm, early_ref, sem)
+    copy.start()
     rows = col_scr.shape[0]
     tall = late[0].shape[0] // PLANE - 1
     chunks = tall // per_pair
     span = float(1 << INDEX_BITS)
 
     def pairs(t, at):
-        if t < len(EARLY):
-            return early_ref[:, t * tall + at : t * tall + at + per_pair, :].reshape(TILE, LANES)
-        ref = late[t - len(EARLY)]
+        k = t - len(LATE)
+        if k >= 0:
+            return early_ref[:, k * tall + at : k * tall + at + per_pair, :].reshape(TILE, LANES)
         return jnp.concatenate(
-            [ref[p * tall + at : p * tall + at + per_pair, :] for p in range(PLANE)], axis=0
+            [late[t][p * tall + at : p * tall + at + per_pair, :] for p in range(PLANE)], axis=0
         )
 
     def tile(t):
         return jnp.concatenate([pairs(t, c * per_pair) for c in range(chunks)], axis=1)
 
-    meta = early_ref[:, len(EARLY) * tall :, :].astype(F32)
-    meta = [meta[:, k, :] for k in range(len(EARLY))] + [ref[PLANE * tall :, :].astype(F32) for ref in late]
-    meta = jnp.concatenate(meta, axis=0)[:, None, :]
-    meta = jnp.broadcast_to(meta, (rows // per_pair, per_pair, LANES)).reshape(rows, LANES)
-    own = (iota((rows, LANES), 0) % per_pair) == (iota((rows, LANES), 1) % per_pair)
-    meta = jnp.where(own, meta, 0.0).astype(BF16)
-    col = dot(meta, piece_weights(iota((LANES, LANES), 0), per_pair))
-    col_scr[...] = col
-    group_scr[...] = jnp.floor(col * (1.0 / span))
-    row_scr[...] = dot_t(piece_weights(iota((8, LANES), 1), per_pair), meta)
-    across_scr[...] = jnp.full(across_scr.shape, -1.0, F32)
-
+    def keys(first, metas):
+        size = len(metas) * TILE
+        at = slice(first * TILE, first * TILE + size)
+        meta = jnp.concatenate(metas, axis=0)[:, None, :]
+        meta = jnp.broadcast_to(meta, (size // per_pair, per_pair, LANES)).reshape(size, LANES)
+        own = (iota((size, LANES), 0) % per_pair) == (iota((size, LANES), 1) % per_pair)
+        meta = jnp.where(own, meta, 0.0).astype(BF16)
+        col = dot(meta, piece_weights(iota((LANES, LANES), 0), per_pair))
+        col_scr[at, :] = col
+        group_scr[at, :] = jnp.floor(col * (1.0 / span))
+        row_scr[:, at] = dot_t(piece_weights(iota((8, LANES), 1), per_pair), meta)
+        across_scr[at, :] = jnp.full((size, LANES), -1.0, F32)
+
+    keys(0, [ref[PLANE * tall :, :].astype(F32) for ref in late])
     down = []
     for i in range(rows // TILE):
+        if i == len(LATE):
+            copy.wait()
+            meta = early_ref[:, len(EARLY) * tall :, :].astype(F32)
+            keys(i, [meta[:, k, :] for k in range(len(EARLY))])
         mine = tile(i)
         row = [row_scr[0:1, i * TILE + b : i * TILE + b + LANES] for b in range(0, TILE, LANES)]
         group = [jnp.floor(r * (1.0 / span)) for r in row]
@@ -279,8 +291,11 @@
 
 ANY = pl.BlockSpec(memory_space=pl.ANY)
 VMEM = pl.BlockSpec(memory_space=pltpu.VMEM)
-FIRST = pltpu.CompilerParams(vmem_limit_bytes=61 * 1024 * 1024)
 LIMIT = pltpu.CompilerParams(vmem_limit_bytes=24 * 1024 * 1024)
+
+
+def in_hbm(*arrays):
+    return [pltpu.with_memory_space_constraint(x, pltpu.HBM) for x in arrays]
 
 
 def shape(dims, dtype):
@@ -320,27 +335,28 @@
     lines = rows // LANES
     tall = width // LANES * per_pair
     block = (PLANE * (tall + 1), LANES)
-    one, pos, meta, flag = pl.pallas_call(
+    *parts, pos, meta, flag, kept = pl.pallas_call(
         functools.partial(first_kernel, members, per_owner, per_pair),
         in_specs=[ANY, ANY, ANY],
-        out_specs=[whole(block), whole((lines, LANES)), whole((members, LANES)), pl.BlockSpec(memory_space=pltpu.SMEM)],
-        out_shape=[
-            shape(block, BF16),
+        out_specs=[whole(block) for _ in SOON]
+        + [whole((lines, LANES)), whole((members, LANES)), pl.BlockSpec(memory_space=pltpu.SMEM), VMEM],
+        out_shape=[shape(block, BF16) for _ in SOON]
+        + [
             shape((lines, LANES), I32),
             shape((members, LANES), F32),
             shape((1,), I32),
+            pltpu.VMEM((rows, width), BF16),
         ],
         scratch_shapes=[
             pltpu.VMEM((lines, LANES), I32),
             pltpu.VMEM((lines, LANES), I32),
-            pltpu.VMEM((rows, width), BF16),
             pltpu.SemaphoreType.DMA((3,)),
         ],
-        compiler_params=FIRST,
+        compiler_params=LIMIT,
         cost_estimate=cost(TILE * rows * width),
         name="send_first",
-    )(cluster_id.reshape(lines, LANES), row_index.reshape(lines, LANES), embeds)
-    got = [to_shift(one, EARLY[0])]
+    )(*in_hbm(cluster_id.reshape(lines, LANES), row_index.reshape(lines, LANES), embeds))
+    got = {dz: to_shift(x, dz) for x, dz in zip(parts, SOON)}
 
     def send(kernel, shifts, more, name):
         return pl.pallas_call(
@@ -352,18 +368,19 @@
             name=name,
         )
 
-    more = send(some_kernel, EARLY[1:3], [], "send_early")(pos, meta, embeds)
-    got += [to_shift(x, dz) for x, dz in zip(more, EARLY[1:3])]
-
-    def late_part(pos, meta, embeds):
-        late = send(late_kernel, (), [shape((PLANE, len(LATE) * tall + META, LANES), BF16)], "send_late")
-        late = in_plane(late(pos, meta, embeds)[0])
+    *parts, late = send(
+        rest_kernel, NEXT, [shape((PLANE, len(LATE) * tall + META, LANES), BF16)], "send_rest"
+    )(pos, meta, kept)
+    got |= {dz: to_shift(x, dz) if dz else x for x, dz in zip(parts, NEXT)}
+
+    def late_part(late):
+        late = in_plane(late)
         parts = pl.pallas_call(
             cut_kernel, out_shape=[shape(block, BF16) for _ in LATE], compiler_params=LIMIT, name="cut"
         )(late)
-        return parts + send(some_kernel, (0,), [], "send_own")(pos, meta, embeds)
-
-    *moving, own = step_of_its_own(late_part, flag, pos, meta, embeds)
+        return parts
+
+    moving = step_of_its_own(late_part, flag, late)
     shifted = [to_shift(x, dz) for x, dz in zip(moving, LATE)]
 
     def last_part(got):
@@ -375,15 +392,18 @@
         )(*got)
         return in_plane(early)
 
-    early = step_of_its_own(last_part, flag, got + [own])
+    early = step_of_its_own(last_part, flag, [got[dz] for dz in EARLY])
     best = pl.pallas_call(
         functools.partial(best_kernel, per_pair),
+        in_specs=[ANY] + [whole(block)] * len(LATE),
         out_shape=shape((members, per_pair), F32),
         scratch_shapes=[
+            pltpu.VMEM((PLANE, len(EARLY) * tall + META, LANES), BF16),
             pltpu.VMEM((rows, LANES), F32),
             pltpu.VMEM((rows, LANES), F32),
             pltpu.VMEM((8, rows), F32),
             pltpu.VMEM((rows, LANES), F32),
+            pltpu.SemaphoreType.DMA,
         ],
         compiler_params=LIMIT,
         cost_estimate=cost(rows * rows * width // 2),

time: 109 us -> 107 us (0.982)
  blocking collectives: 39 us -> 68.9 us
  waiting for transfers between devices: 17.8 us -> 0.02 us
  Pallas kernels: 26.5 us -> 18.6 us
  starting transfers between devices: 24.6 us -> 18.6 us
    all_to_all x1 -> x2, blocking collectives: 25.9 us -> 53.5 us  [in_plane(): lax.all_to_all(rows, 'member', split_axis=0, concat_axis=0, tiled=True, a...]
    all_to_all x1 -> x0, waiting for transfers between devices: 17.8 us -> none  [in_plane(): lax.all_to_all(rows, 'member', split_axis=0, concat_axis=0, tiled=True, a...]
    pallas_call x4 -> x2, Pallas kernels: 19.1 us -> 11.9 us  [the longest x1 6.15 us: on_device(): send(rest_kernel, NEXT, [shape((PLANE, len(LATE) * tall + META, LANES), B...]
    all_to_all x1 -> x0, starting transfers between devices: 5.99 us -> none  [in_plane(): lax.all_to_all(rows, 'member', split_axis=0, concat_axis=0, tiled=True, a...]
    all_to_all x1, blocking collectives: 13.1 us -> 15.4 us  [on_device(): lax.all_to_all(best, 'member', split_axis=0, concat_axis=0, tiled=True)]
  transfers between devices with their start and end apart: 8 -> 7, of which waited for: 1 -> 0; matrix products, arithmetic and copies ran while one was open for 0% -> 0% of each run, Pallas kernels for 15% -> 8%
where the time goes in v4:
time: 107 us
  blocking collectives  68.9 us (64%)
  Pallas kernels  18.6 us (17%)
  starting transfers between devices  18.6 us (17%)
    all_to_all x2, blocking collectives, in_plane(): lax.all_to_all(rows, 'member', split_axis=0, concat_axis=0, tiled=True, a...  53.5 us
    ppermute x7, starting transfers between devices, to_shift(): return lax.ppermute(rows, 'member', pairs)  18.6 us
    all_to_all x1, blocking collectives, on_device(): lax.all_to_all(best, 'member', split_axis=0, concat_axis=0, tiled=True)  15.4 us
    pallas_call x1, Pallas kernels, on_device(): send(rest_kernel, NEXT, [shape((PLANE, len(LATE) * tall + META, LANES), B...  6.15 us
    pallas_call x1, Pallas kernels, on_device(): pl.pallas_call(functools.partial(best_kernel, per_pair), in_specs=[ANY] +...  5.7 us
    pallas_call x1, Pallas kernels, on_device(): pl.pallas_call(functools.partial(first_kernel, members, per_owner, per_pa...  3.39 us
  transfers between devices with their start and end apart: 7, of which 0 were waited for; matrix products, arithmetic and copies ran while one was open for 0% of the time, Pallas kernels for 8%

profile of v4, /device:TPU:1, one launch (start us, length us, event | category | flops | bytes accessed | tf_op | source)
XLA Modules:
  0.0 106.9 jit_solution(10858930043038628176)
XLA Ops:
  0.0 3.4 %send_first.1 = (bf16[1544,128]{1,0:T(8,128)(2,1)S(1)}, s32[16,128]{1,0:T(8,128)S(1)}, f32[64,128]{1,0:T(8,128)S(1)}, s32[1]{0:T(128)}, bf16[2048,768]{1,0:T(8,128)(2,1)S(1)}) custom-call(s32[16,128]{1,0:T(8,128)} %bitcast.10, s32[16,128]{1,0:T(8,128)} %bitcast.11, bf16[2048,768]{1,0:T(8,128)(2,1)} %emb_hbm.1), custom_call_target="tpu_custom_call" | custom-call | flops 805306368 | bytes 8388608 | tf_op jit(solution)/shard_map/send_first/pallas_call | solution.py:338
  3.4 7.8 %collective-permute-start = (bf16[1544,128]{1,0:T(8,128)(2,1)S(1)}, bf16[1544,128]{1,0:T(8,128)(2,1)S(1)}, u32[]{:S(2)}, u32[]{:S(2)}) collective-permute-start(bf16[1544,128]{1,0:T(8,128)(2,1)S(1)} %get-tuple-element.35), channel_id=1, source_target_pairs={{0,8},{1,9},{2,10},{3,11},{4,12},{5,13},{6,14},{7,15},{8,0},{9,1},... | collective-permute-start | bytes 1185800 | tf_op jit(solution)/shard_map/ppermute | solution.py:315
  11.2 6.2 %send_rest.1 = (bf16[1544,128]{1,0:T(8,128)(2,1)S(1)}, bf16[1544,128]{1,0:T(8,128)(2,1)S(1)}, bf16[1544,128]{1,0:T(8,128)(2,1)S(1)}, bf16[8,776,128]{2,1,0:T(8,128)(2,1)S(1)}) custom-call(s32[16,128]{1,0:T(8,128)S(1)} %get-tuple-element.36.pos_ref, f32[64,128]{1,0:T(8,128)S(1)} %get-tuple-element.37.meta_ref, bf16[2048,768]{1,0:T(8,128)(2,1)S(1)} %get-tuple-element.38.emb_ref), custom_call_target="tpu_custom_call" | custom-call | flops 2415919104 | bytes 8388608 | tf_op jit(solution)/shard_map/send_rest/pallas_call | solution.py:371
  17.4 1.7 %collective-permute-start.1 = (bf16[1544,128]{1,0:T(8,128)(2,1)S(1)}, bf16[1544,128]{1,0:T(8,128)(2,1)S(1)}, u32[]{:S(2)}, u32[]{:S(2)}) collective-permute-start(bf16[1544,128]{1,0:T(8,128)(2,1)S(1)} %get-tuple-element.39), channel_id=1, source_target_pairs={{0,6},{1,7},{2,8},{3,9},{4,10},{5,11},{6,12},{7,13},{8,14},{9,15},... | collective-permute-start | bytes 1185800 | tf_op jit(solution)/shard_map/ppermute | solution.py:315
  19.1 2.8 %collective-permute-start.2 = (bf16[1544,128]{1,0:T(8,128)(2,1)S(1)}, bf16[1544,128]{1,0:T(8,128)(2,1)}, u32[]{:S(2)}, u32[]{:S(2)}) collective-permute-start(bf16[1544,128]{1,0:T(8,128)(2,1)S(1)} %get-tuple-element.40), channel_id=1, source_target_pairs={{0,10},{1,11},{2,12},{3,13},{4,14},{5,15},{6,0},{7,1},{8,2},{9,3},... | collective-permute-start | bytes 1185800 | tf_op jit(solution)/shard_map/ppermute | solution.py:315
  22.6 28.6 %conditional.3 = ((bf16[1544,128]{1,0:T(8,128)(2,1)}, bf16[1544,128]{1,0:T(8,128)(2,1)}, bf16[1544,128]{1,0:T(8,128)(2,1)}, bf16[1544,128]{1,0:T(8,128)(2,1)})) conditional(s32[]{:T(128)} %bitcast.2, () %tuple.20, bf16[8,776,128]{2,1,0:T(8,128)(2,1)S(1)} %get-tuple-element.42), branch_computations={%region_2.0_spmd, %region_3.0_spmd} | conditional | bytes 3178504 | solution.py:327
  22.6 27.3 %all_to_all.20.got_ref = bf16[8,776,128]{2,1,0:T(8,128)(2,1)S(1)} all-to-all(bf16[8,776,128]{2,1,0:T(8,128)(2,1)S(1)} %param.3), channel_id=1, replica_groups={{0,1,16,17,32,33,48,49},{2,3,18,19,34,35,50,51},{4,5,20,21,36,37,52,53}..., dimensions={0} | all-to-all | bytes 3178496 | tf_op jit(solution)/shard_map/cond/branch_1_fun/all_to_all | solution.py:321
  50.0 1.3 %cut.1 = (bf16[1544,128]{1,0:T(8,128)(2,1)}, bf16[1544,128]{1,0:T(8,128)(2,1)}, bf16[1544,128]{1,0:T(8,128)(2,1)}, bf16[1544,128]{1,0:T(8,128)(2,1)}) custom-call(bf16[8,776,128]{2,1,0:T(8,128)(2,1)S(1)} %all_to_all.20.got_ref), custom_call_target="tpu_custom_call" | custom-call | tf_op jit(solution)/shard_map/cond/branch_1_fun/cut/pallas_call | solution.py:378
  51.2 1.3 %collective-permute-start.3 = (bf16[1544,128]{1,0:T(8,128)(2,1)}, bf16[1544,128]{1,0:T(8,128)(2,1)S(1)}, u32[]{:S(2)}, u32[]{:S(2)}) collective-permute-start(bf16[1544,128]{1,0:T(8,128)(2,1)} %get-tuple-element.43), channel_id=1, source_target_pairs={{0,4},{1,5},{2,6},{3,7},{4,8},{5,9},{6,10},{7,11},{8,12},{9,13},{1... | collective-permute-start | bytes 1185800 | tf_op jit(solution)/shard_map/ppermute | solution.py:315
  52.5 2.3 %collective-permute-start.4 = (bf16[1544,128]{1,0:T(8,128)(2,1)}, bf16[1544,128]{1,0:T(8,128)(2,1)S(1)}, u32[]{:S(2)}, u32[]{:S(2)}) collective-permute-start(bf16[1544,128]{1,0:T(8,128)(2,1)} %get-tuple-element.44), channel_id=1, source_target_pairs={{0,12},{1,13},{2,14},{3,15},{4,0},{5,1},{6,2},{7,3},{8,4},{9,5},{1... | collective-permute-start | bytes 1185800 | tf_op jit(solution)/shard_map/ppermute | solution.py:315
  54.8 0.0 collective-permute-done
  54.8 0.8 collective-permute-start.5
  55.7 0.0 collective-permute-done.1
  55.7 1.8 %collective-permute-start.6 = (bf16[1544,128]{1,0:T(8,128)(2,1)}, bf16[1544,128]{1,0:T(8,128)(2,1)S(1)}, u32[]{:S(2)}, u32[]{:S(2)}) collective-permute-start(bf16[1544,128]{1,0:T(8,128)(2,1)} %get-tuple-element.46), channel_id=1, source_target_pairs={{0,14},{1,15},{2,0},{3,1},{4,2},{5,3},{6,4},{7,5},{8,6},{9,7},{10,... | collective-permute-start | bytes 1185800 | tf_op jit(solution)/shard_map/ppermute | solution.py:315
  57.5 0.0 collective-permute-done.2
  57.5 27.3 %conditional.2 = (bf16[8,776,128]{2,1,0:T(8,128)(2,1)}) conditional(s32[]{:T(128)} %bitcast.2, () %tuple.18, (bf16[1544,128]{1,0:T(8,128)(2,1)S(1)}, bf16[1544,128]{1,0:T(8,128)(2,1)S(1)}, bf16[1544,128]{1,0:T(8,128)(2,1)}, bf16[1544,128]{1,0:T(8,128)(2,1)S(1)}) %tuple.19), branch_computations={%region_0.0_spmd, %region_1.0_spmd} | conditional | bytes 3178504 | solution.py:327
  57.5 1.1 %merge.1 = bf16[8,776,128]{2,1,0:T(8,128)(2,1)S(1)} custom-call(bf16[1544,128]{1,0:T(8,128)(2,1)S(1)} %get-tuple-element.17.refs_0_, bf16[1544,128]{1,0:T(8,128)(2,1)S(1)} %get-tuple-element.18.refs_1_, bf16[1544,128]{1,0:T(8,128)(2,1)} %get-tuple-element.19.refs_2_, bf16[1544,128]{1,0:T(8,128)(2,1)S(1)} %get-tuple-element.20.refs_3_), custom_call_target="tpu_custom_call" | custom-call | tf_op jit(solution)/shard_map/cond/branch_1_fun/merge/pallas_call | solution.py:387
  58.6 26.2 %all_to_all.19 = bf16[8,776,128]{2,1,0:T(8,128)(2,1)} all-to-all(bf16[8,776,128]{2,1,0:T(8,128)(2,1)S(1)} %merge.1), channel_id=1, replica_groups={{0,1,16,17,32,33,48,49},{2,3,18,19,34,35,50,51},{4,5,20,21,36,37,52,53}..., dimensions={0} | all-to-all | bytes 3178496 | tf_op jit(solution)/shard_map/cond/branch_1_fun/all_to_all | solution.py:321
  84.8 0.0 collective-permute-done.3.refs_0_
  84.8 0.0 collective-permute-done.4.refs_1_
  84.8 0.0 collective-permute-done.6.refs_3_
  84.8 5.7 %best.1 = f32[64,32]{1,0:T(8,128)S(1)} custom-call(bf16[8,776,128]{2,1,0:T(8,128)(2,1)} %get-tuple-element.55.early_hbm, bf16[1544,128]{1,0:T(8,128)(2,1)S(1)} %collective-permute-done.3.refs_0_, bf16[1544,128]{1,0:T(8,128)(2,1)S(1)} %collective-permute-done.4.refs_1_, bf16[1544,128]{1,0:T(8,128)(2,1)S(1)} %collective-permute-done.5.refs_2_, ...), custom_call_target="tpu_custom_call" | custom-call | flops 3221225472 | bytes 8388608 | tf_op jit(solution)/shard_map/best/pallas_call | solution.py:396
  90.5 15.4 %all_to_all.21 = f32[64,1,32]{2,1,0:T(1,128)S(1)} all-to-all(f32[64,1,32]{2,1,0:T(1,128)S(1)} %bitcast.9), channel_id=1, replica_groups=mesh['outer'=4,'member'=64] {'member'}, dimensions={0} | all-to-all | bytes 16384 | tf_op jit(solution)/shard_map/all_to_all | solution.py:412
  105.9 1.0 home.1
  (1 shorter events, 0.0 us)
Async XLA Ops:
  3.4 51.4 %collective-permute-start = (bf16[1544,128]{1,0:T(8,128)(2,1)S(1)}, bf16[1544,128]{1,0:T(8,128)(2,1)S(1)}, u32[]{:S(2)}, u32[]{:S(2)}) collective-permute-start(bf16[1544,128]{1,0:T(8,128)(2,1)S(1)} %get-tuple-element.35), channel_id=1, source_target_pairs={{0,8},{1,9},{2,10},{3,11},{4,12},{5,13},{6,14},{7,15},{8,0},{9,1},... | collective-permute-start | bytes 1185800 | tf_op jit(solution)/shard_map/ppermute | solution.py:315
  17.4 38.3 %collective-permute-start.1 = (bf16[1544,128]{1,0:T(8,128)(2,1)S(1)}, bf16[1544,128]{1,0:T(8,128)(2,1)S(1)}, u32[]{:S(2)}, u32[]{:S(2)}) collective-permute-start(bf16[1544,128]{1,0:T(8,128)(2,1)S(1)} %get-tuple-element.39), channel_id=1, source_target_pairs={{0,6},{1,7},{2,8},{3,9},{4,10},{5,11},{6,12},{7,13},{8,14},{9,15},... | collective-permute-start | bytes 1185800 | tf_op jit(solution)/shard_map/ppermute | solution.py:315
  19.1 38.4 %collective-permute-start.2 = (bf16[1544,128]{1,0:T(8,128)(2,1)S(1)}, bf16[1544,128]{1,0:T(8,128)(2,1)}, u32[]{:S(2)}, u32[]{:S(2)}) collective-permute-start(bf16[1544,128]{1,0:T(8,128)(2,1)S(1)} %get-tuple-element.40), channel_id=1, source_target_pairs={{0,10},{1,11},{2,12},{3,13},{4,14},{5,15},{6,0},{7,1},{8,2},{9,3},... | collective-permute-start | bytes 1185800 | tf_op jit(solution)/shard_map/ppermute | solution.py:315
  51.2 33.5 %collective-permute-start.3 = (bf16[1544,128]{1,0:T(8,128)(2,1)}, bf16[1544,128]{1,0:T(8,128)(2,1)S(1)}, u32[]{:S(2)}, u32[]{:S(2)}) collective-permute-start(bf16[1544,128]{1,0:T(8,128)(2,1)} %get-tuple-element.43), channel_id=1, source_target_pairs={{0,4},{1,5},{2,6},{3,7},{4,8},{5,9},{6,10},{7,11},{8,12},{9,13},{1... | collective-permute-start | bytes 1185800 | tf_op jit(solution)/shard_map/ppermute | solution.py:315
  52.5 32.3 %collective-permute-start.4 = (bf16[1544,128]{1,0:T(8,128)(2,1)}, bf16[1544,128]{1,0:T(8,128)(2,1)S(1)}, u32[]{:S(2)}, u32[]{:S(2)}) collective-permute-start(bf16[1544,128]{1,0:T(8,128)(2,1)} %get-tuple-element.44), channel_id=1, source_target_pairs={{0,12},{1,13},{2,14},{3,15},{4,0},{5,1},{6,2},{7,3},{8,4},{9,5},{1... | collective-permute-start | bytes 1185800 | tf_op jit(solution)/shard_map/ppermute | solution.py:315
  54.8 30.0 %collective-permute-start.5 = (bf16[1544,128]{1,0:T(8,128)(2,1)}, bf16[1544,128]{1,0:T(8,128)(2,1)S(1)}, u32[]{:S(2)}, u32[]{:S(2)}) collective-permute-start(bf16[1544,128]{1,0:T(8,128)(2,1)} %get-tuple-element.45), channel_id=1, source_target_pairs={{0,2},{1,3},{2,4},{3,5},{4,6},{5,7},{6,8},{7,9},{8,10},{9,11},{10,... | collective-permute-start | bytes 1185800 | tf_op jit(solution)/shard_map/ppermute | solution.py:315
  55.7 29.1 %collective-permute-start.6 = (bf16[1544,128]{1,0:T(8,128)(2,1)}, bf16[1544,128]{1,0:T(8,128)(2,1)S(1)}, u32[]{:S(2)}, u32[]{:S(2)}) collective-permute-start(bf16[1544,128]{1,0:T(8,128)(2,1)} %get-tuple-element.46), channel_id=1, source_target_pairs={{0,14},{1,15},{2,0},{3,1},{4,2},{5,3},{6,4},{7,5},{8,6},{9,7},{10,... | collective-permute-start | bytes 1185800 | tf_op jit(solution)/shard_map/ppermute | solution.py:315

commit v5 on v4

--- a/solution.py
+++ b/solution.py
@@ -13,10 +13,11 @@
 META = 8
 TILE = 256
 NZ, CORES, PLANE = 8, 2, 8
-EARLY = (4, 3, 5, 0)
-LATE = (2, 6, 1, 7)
-SOON, NEXT = (4,), (3, 5, 0)
-ORDER = LATE + EARLY
+EARLY = (4, 3, 5)
+LATE = (2, 6, 1, 7, 0)
+SOON, NEXT = (4,), (3, 5)
+ORDER = (2, 6, 0, 4, 3, 5, 1, 7)
+MID = range(3, 6)
 BF16, F32, I32 = jnp.bfloat16, jnp.float32, jnp.int32
 
 
@@ -118,8 +119,12 @@
     *outs, pos_ref, meta_ref, flag_ref, emb_ref, cid_ref, idx_ref, sem = refs
     copies = [
         pltpu.make_async_copy(src, dst, sem.at[n])
-        for n, (src, dst) in enumerate(((cid_hbm, cid_ref), (idx_hbm, idx_ref), (emb_hbm, emb_ref)))
+        for n, (src, dst) in enumerate(((cid_hbm, cid_ref), (idx_hbm, idx_ref)))
     ]
+    half = emb_ref.shape[0] // 2
+    for n in range(2):
+        at = pl.ds(n * half, half)
+        copies.append(pltpu.make_async_copy(emb_hbm.at[at], emb_ref.at[at], sem.at[2 + n]))
     for copy in copies:
         copy.start()
     copies[0].wait()
@@ -129,8 +134,13 @@
     meta_ref[...] = meta
     flag_ref[0] = 1
     goal = place(pos, per_pair, SOON, False)
+    pick = picked(goal, 0, PLANE * per_pair)
     copies[2].wait()
-    put_blocks(outs, SOON, goal, meta_ref, emb_ref, per_pair)
+    moved = dot(pick[:, :half], emb_ref[:half, :])
+    copies[3].wait()
+    moved = moved + dot(pick[:, half:], emb_ref[half:, :])
+    shift = SOON[0]
+    put_block(outs[0], scaled(moved), meta[shift * PLANE : (shift + 1) * PLANE])
 
 
 def some_kernel(per_pair, shifts, pos_ref, meta_ref, emb_ref, *outs):
@@ -144,7 +154,7 @@
     goal = place(wide_row(pos_ref), per_pair, LATE, True)
     some = len(LATE) * per_pair
     tall = emb_ref.shape[1] // LANES * per_pair
-    step = 512 // some
+    step = 4
     for p0 in range(0, PLANE, step):
         unit = scaled(dot(picked(goal, p0 * some, step * some), emb_ref[...]))
         for p in range(p0, p0 + step):
@@ -182,22 +192,26 @@
     return value.astype(BF16)
 
 
-def best_kernel(per_pair, early_hbm, *refs):
-    *late, out_ref, early_ref, col_scr, group_scr, row_scr, across_scr, sem = refs
+def best_kernel(per_pair, last, early_hbm, *refs):
+    *blocks, out_ref, early_ref, col_scr, group_scr, row_scr, across_scr, sem = refs
+    seen_ref = blocks.pop() if last else None
     copy = pltpu.make_async_copy(early_hbm, early_ref, sem)
     copy.start()
-    rows = col_scr.shape[0]
-    tall = late[0].shape[0] // PLANE - 1
+    tall = blocks[0].shape[0] // PLANE - 1
     chunks = tall // per_pair
     span = float(1 << INDEX_BITS)
+    tiles = col_scr.shape[0] // TILE
+    across_scr[...] = jnp.full(across_scr.shape, -1.0, F32)
+
+    def block(t):
+        return blocks[t if t < MID.start else t - len(MID)]
 
     def pairs(t, at):
-        k = t - len(LATE)
-        if k >= 0:
-            return early_ref[:, k * tall + at : k * tall + at + per_pair, :].reshape(TILE, LANES)
-        return jnp.concatenate(
-            [late[t][p * tall + at : p * tall + at + per_pair, :] for p in range(PLANE)], axis=0
-        )
+        if t in MID:
+            at += (t - MID.start) * tall
+            return early_ref[:, at : at + per_pair, :].reshape(TILE, LANES)
+        ref = block(t)
+        return jnp.concatenate([ref[p * tall + at : p * tall + at + per_pair, :] for p in range(PLANE)], axis=0)
 
     def tile(t):
         return jnp.concatenate([pairs(t, c * per_pair) for c in range(chunks)], axis=1)
@@ -213,59 +227,68 @@
         col_scr[at, :] = col
         group_scr[at, :] = jnp.floor(col * (1.0 / span))
         row_scr[:, at] = dot_t(piece_weights(iota((8, LANES), 1), per_pair), meta)
-        across_scr[at, :] = jnp.full((size, LANES), -1.0, F32)
-
-    keys(0, [ref[PLANE * tall :, :].astype(F32) for ref in late])
-    down = []
-    for i in range(rows // TILE):
-        if i == len(LATE):
-            copy.wait()
-            meta = early_ref[:, len(EARLY) * tall :, :].astype(F32)
-            keys(i, [meta[:, k, :] for k in range(len(EARLY))])
-        mine = tile(i)
-        row = [row_scr[0:1, i * TILE + b : i * TILE + b + LANES] for b in range(0, TILE, LANES)]
-        group = [jnp.floor(r * (1.0 / span)) for r in row]
-        best = [jnp.full((1, LANES), -1.0, F32) for _ in row]
-        for j in range(i + 1):
-            at = slice(j * TILE, (j + 1) * TILE)
-            scores = dot_t(tile(j), mine)
-            col, col_group = col_scr[at, :], group_scr[at, :]
-            across = across_scr[at, :]
-            for b in range(len(row)):
-                part = jnp.where(col_group == group[b], scores[:, b * LANES : (b + 1) * LANES], -1.0)
-                before = col < row[b]
-                best[b] = jnp.maximum(best[b], jnp.max(jnp.where(before, part, -1.0), axis=0, keepdims=True))
-                if j < i:
-                    across = jnp.maximum(across, jnp.where(before, -1.0, part))
+
+    best = {}
+
+    def compare(i, j):
+        at = slice(j * TILE, (j + 1) * TILE)
+        scores = dot_t(tile(j), tile(i))
+        col, col_group = col_scr[at, :], group_scr[at, :]
+        across = across_scr[at, :]
+        for b in range(TILE // LANES):
+            n = i * (TILE // LANES) + b
+            row = row_scr[0:1, n * LANES : (n + 1) * LANES]
+            group = jnp.floor(row * (1.0 / span))
+            part = jnp.where(col_group == group, scores[:, b * LANES : (b + 1) * LANES], -1.0)
+            before = col < row
+            high = jnp.max(jnp.where(before, part, -1.0), axis=0, keepdims=True)
+            best[n] = jnp.maximum(best[n], high) if n in best else high
             if j < i:
-                across_scr[at, :] = across
-        down += best
-
-    best = [
-        jnp.maximum(
-            down[b], jnp.max(across_scr[b * LANES : (b + 1) * LANES, :].T, axis=0, keepdims=True)
-        )
-        for b in range(rows // LANES)
-    ]
-    best = jnp.concatenate(best, axis=1)
-    homes = out_ref.shape[0]
-    place_in = iota((1, rows), 1)
-    slot = place_in // TILE
-    plane = place_in % TILE // per_pair
-    shift = jnp.zeros((1, rows), I32)
-    for t, dz in enumerate(ORDER):
-        shift = jnp.where(slot == t, dz, shift)
-    z = (my_z() + NZ - shift) % NZ
-    home = plane // CORES * (CORES * NZ) + z * CORES + plane % CORES
-    to = (iota((homes, rows), 0) == home).astype(BF16)
-    own = iota((per_pair, rows), 0) == place_in % per_pair
-    rest = jnp.where(own, best, 0.0)
-    total = jnp.zeros(out_ref.shape, F32)
-    for _ in range(3):
-        part = rest.astype(BF16)
-        rest = rest - part.astype(F32)
-        total = total + dot_t(to, part)
-    out_ref[...] = total
+                across = jnp.maximum(across, jnp.where(before, -1.0, part))
+        if j < i:
+            across_scr[at, :] = across
+
+    new = range(MID.stop, tiles) if last else range(tiles)
+    todo = [(i, j) for i in new for j in range(i + 1)]
+    keys(0, [block(t)[PLANE * tall :, :].astype(F32) for t in range(MID.start)])
+    if last:
+        keys(MID.stop, [block(t)[PLANE * tall :, :].astype(F32) for t in new])
+    for i, j in todo:
+        if i not in MID and j not in MID:
+            compare(i, j)
+    copy.wait()
+    meta = early_ref[:, len(MID) * tall :, :].astype(F32)
+    keys(MID.start, [meta[:, k, :] for k in range(len(MID))])
+    for i, j in todo:
+        if i in MID or j in MID:
+            compare(i, j)
+
+    total = None
+    for t in range(tiles):
+        parts = []
+        for b in range(TILE // LANES):
+            n = t * (TILE // LANES) + b
+            at = slice(n * LANES, (n + 1) * LANES)
+            part = jnp.max(across_scr[at, :].T, axis=0, keepdims=True)
+            part = jnp.maximum(part, best[n] if n in best else seen_ref[0:1, at])
+            parts.append(part)
+            if not last:
+                out_ref[0:1, at] = part
+        if last:
+            place_in = iota((1, TILE), 1)
+            plane = place_in // per_pair
+            z = (my_z() + NZ - ORDER[t]) % NZ
+            home = plane // CORES * (CORES * NZ) + z * CORES + plane % CORES
+            to = (iota((out_ref.shape[0], TILE), 0) == home).astype(BF16)
+            own = iota((per_pair, TILE), 0) == place_in % per_pair
+            rest = jnp.where(own, jnp.concatenate(parts, axis=1), 0.0)
+            for _ in range(3):
+                piece = rest.astype(BF16)
+                rest = rest - piece.astype(F32)
+                add = dot_t(to, piece)
+                total = add if total is None else total + add
+    if last:
+        out_ref[...] = total
 
 
 def home_kernel(ret_ref, pos_ref, out_ref):
@@ -350,7 +373,7 @@
         scratch_shapes=[
             pltpu.VMEM((lines, LANES), I32),
             pltpu.VMEM((lines, LANES), I32),
-            pltpu.SemaphoreType.DMA((3,)),
+            pltpu.SemaphoreType.DMA((4,)),
         ],
         compiler_params=LIMIT,
         cost_estimate=cost(TILE * rows * width),
@@ -371,7 +394,7 @@
     *parts, late = send(
         rest_kernel, NEXT, [shape((PLANE, len(LATE) * tall + META, LANES), BF16)], "send_rest"
     )(pos, meta, kept)
-    got |= {dz: to_shift(x, dz) if dz else x for x, dz in zip(parts, NEXT)}
+    got |= {dz: to_shift(x, dz) for x, dz in zip(parts, NEXT)}
 
     def late_part(late):
         late = in_plane(late)
@@ -381,7 +404,7 @@
         return parts
 
     moving = step_of_its_own(late_part, flag, late)
-    shifted = [to_shift(x, dz) for x, dz in zip(moving, LATE)]
+    shifted = [to_shift(x, dz) if dz else x for x, dz in zip(moving, LATE)]
 
     def last_part(got):
         early = pl.pallas_call(
@@ -393,22 +416,30 @@
         return in_plane(early)
 
     early = step_of_its_own(last_part, flag, [got[dz] for dz in EARLY])
-    best = pl.pallas_call(
-        functools.partial(best_kernel, per_pair),
-        in_specs=[ANY] + [whole(block)] * len(LATE),
-        out_shape=shape((members, per_pair), F32),
-        scratch_shapes=[
-            pltpu.VMEM((PLANE, len(EARLY) * tall + META, LANES), BF16),
-            pltpu.VMEM((rows, LANES), F32),
-            pltpu.VMEM((rows, LANES), F32),
-            pltpu.VMEM((8, rows), F32),
-            pltpu.VMEM((rows, LANES), F32),
-            pltpu.SemaphoreType.DMA,
-        ],
-        compiler_params=LIMIT,
-        cost_estimate=cost(rows * rows * width // 2),
-        name="best",
-    )(early, *shifted)
+    shifted = dict(zip(LATE, shifted))
+
+    def best_of(last, more, out, tiles, name):
+        blocks = [shifted[dz] for n, dz in enumerate(ORDER[:tiles]) if n not in MID] + more
+        size = tiles * TILE
+        return pl.pallas_call(
+            functools.partial(best_kernel, per_pair, last),
+            in_specs=[ANY] + [whole(x.shape) for x in blocks],
+            out_shape=shape(out, F32),
+            scratch_shapes=[
+                pltpu.VMEM((PLANE, len(EARLY) * tall + META, LANES), BF16),
+                pltpu.VMEM((size, LANES), F32),
+                pltpu.VMEM((size, LANES), F32),
+                pltpu.VMEM((8, size), F32),
+                pltpu.VMEM((size, LANES), F32),
+                pltpu.SemaphoreType.DMA,
+            ],
+            compiler_params=LIMIT,
+            cost_estimate=cost(size * size * width // 2),
+            name=name,
+        )(early, *blocks)
+
+    seen = best_of(False, [], (8, MID.stop * TILE), MID.stop, "best_early")
+    best = best_of(True, [seen], (members, per_pair), len(ORDER), "best_last")
     back = lax.all_to_all(best, "member", split_axis=0, concat_axis=0, tiled=True)
     nearest = pl.pallas_call(
         home_kernel,

time: 107 us -> 105 us (0.981)
  blocking collectives: 68.9 us -> 65.8 us
  Pallas kernels: 18.6 us -> 19.8 us
    all_to_all x1, blocking collectives: 15.4 us -> 13.5 us  [on_device(): lax.all_to_all(best, 'member', split_axis=0, concat_axis=0, tiled=True)]
    all_to_all x2, blocking collectives: 53.5 us -> 52.3 us  [in_plane(): lax.all_to_all(rows, 'member', split_axis=0, concat_axis=0, tiled=True, a...]
    pallas_call x1 -> x2, Pallas kernels: 5.7 us -> 6.67 us  [best_of(): pl.pallas_call(functools.partial(best_kernel, per_pair, last), in_specs=[...]
  transfers between devices with their start and end apart: 7 -> 7, of which waited for: 0 -> 0; matrix products, arithmetic and copies ran while one was open for 0% -> 0% of each run, Pallas kernels for 8% -> 12%
where the time goes in v5:
time: 105 us
  blocking collectives  65.8 us (63%)
  Pallas kernels  19.8 us (19%)
  starting transfers between devices  18.6 us (18%)
    all_to_all x2, blocking collectives, in_plane(): lax.all_to_all(rows, 'member', split_axis=0, concat_axis=0, tiled=True, a...  52.3 us
    ppermute x7, starting transfers between devices, to_shift(): return lax.ppermute(rows, 'member', pairs)  18.6 us
    all_to_all x1, blocking collectives, on_device(): lax.all_to_all(best, 'member', split_axis=0, concat_axis=0, tiled=True)  13.5 us
    pallas_call x2, Pallas kernels, best_of(): pl.pallas_call(functools.partial(best_kernel, per_pair, last), in_specs=[...  6.67 us
    pallas_call x1, Pallas kernels, on_device(): send(rest_kernel, NEXT, [shape((PLANE, len(LATE) * tall + META, LANES), B...  6.18 us
    pallas_call x1, Pallas kernels, on_device(): pl.pallas_call(functools.partial(first_kernel, members, per_owner, per_pa...  3.19 us
  transfers between devices with their start and end apart: 7, of which 0 were waited for; matrix products, arithmetic and copies ran while one was open for 0% of the time, Pallas kernels for 12%

profile of v5, /device:TPU:1, one launch (start us, length us, event | category | flops | bytes accessed | tf_op | source)
XLA Modules:
  0.0 105.1 jit_solution(11283251126332073789)
XLA Ops:
  0.0 3.2 %send_first.1 = (bf16[1544,128]{1,0:T(8,128)(2,1)S(1)}, s32[16,128]{1,0:T(8,128)S(1)}, f32[64,128]{1,0:T(8,128)S(1)}, s32[1]{0:T(128)}, bf16[2048,768]{1,0:T(8,128)(2,1)S(1)}) custom-call(s32[16,128]{1,0:T(8,128)} %bitcast.10, s32[16,128]{1,0:T(8,128)} %bitcast.11, bf16[2048,768]{1,0:T(8,128)(2,1)} %emb_hbm.1), custom_call_target="tpu_custom_call" | custom-call | flops 805306368 | bytes 8388608 | tf_op jit(solution)/shard_map/send_first/pallas_call | solution.py:361
  3.2 7.8 %collective-permute-start = (bf16[1544,128]{1,0:T(8,128)(2,1)S(1)}, bf16[1544,128]{1,0:T(8,128)(2,1)}, u32[]{:S(2)}, u32[]{:S(2)}) collective-permute-start(bf16[1544,128]{1,0:T(8,128)(2,1)S(1)} %get-tuple-element.32), channel_id=1, source_target_pairs={{0,8},{1,9},{2,10},{3,11},{4,12},{5,13},{6,14},{7,15},{8,0},{9,1},... | collective-permute-start | bytes 1185800 | tf_op jit(solution)/shard_map/ppermute | solution.py:338
  11.0 6.2 %send_rest.1 = (bf16[1544,128]{1,0:T(8,128)(2,1)S(1)}, bf16[1544,128]{1,0:T(8,128)(2,1)S(1)}, bf16[8,968,128]{2,1,0:T(8,128)(2,1)S(1)}) custom-call(s32[16,128]{1,0:T(8,128)S(1)} %get-tuple-element.33.pos_ref, f32[64,128]{1,0:T(8,128)S(1)} %get-tuple-element.34.meta_ref, bf16[2048,768]{1,0:T(8,128)(2,1)S(1)} %get-tuple-element.35.emb_ref), custom_call_target="tpu_custom_call" | custom-call | flops 1610612736 | bytes 8388608 | tf_op jit(solution)/shard_map/send_rest/pallas_call | solution.py:394
  17.2 1.7 %collective-permute-start.1 = (bf16[1544,128]{1,0:T(8,128)(2,1)S(1)}, bf16[1544,128]{1,0:T(8,128)(2,1)}, u32[]{:S(2)}, u32[]{:S(2)}) collective-permute-start(bf16[1544,128]{1,0:T(8,128)(2,1)S(1)} %get-tuple-element.36), channel_id=1, source_target_pairs={{0,6},{1,7},{2,8},{3,9},{4,10},{5,11},{6,12},{7,13},{8,14},{9,15},... | collective-permute-start | bytes 1185800 | tf_op jit(solution)/shard_map/ppermute | solution.py:338
  18.9 2.8 %collective-permute-start.2 = (bf16[1544,128]{1,0:T(8,128)(2,1)S(1)}, bf16[1544,128]{1,0:T(8,128)(2,1)}, u32[]{:S(2)}, u32[]{:S(2)}) collective-permute-start(bf16[1544,128]{1,0:T(8,128)(2,1)S(1)} %get-tuple-element.37), channel_id=1, source_target_pairs={{0,10},{1,11},{2,12},{3,13},{4,14},{5,15},{6,0},{7,1},{8,2},{9,3},... | collective-permute-start | bytes 1185800 | tf_op jit(solution)/shard_map/ppermute | solution.py:338
  22.4 32.9 %conditional.3 = ((bf16[1544,128]{1,0:T(8,128)(2,1)}, bf16[1544,128]{1,0:T(8,128)(2,1)}, bf16[1544,128]{1,0:T(8,128)(2,1)}, bf16[1544,128]{1,0:T(8,128)(2,1)}, bf16[1544,128]{1,0:T(8,128)(2,1)})) conditional(s32[]{:T(128)} %bitcast.2, () %tuple.20, bf16[8,968,128]{2,1,0:T(8,128)(2,1)S(1)} %get-tuple-element.38), branch_computations={%region_2.0_spmd, %region_3.0_spmd} | conditional | bytes 3964936 | solution.py:350
  22.4 31.4 %all_to_all.20.got_ref = bf16[8,968,128]{2,1,0:T(8,128)(2,1)S(1)} all-to-all(bf16[8,968,128]{2,1,0:T(8,128)(2,1)S(1)} %param.3), channel_id=1, replica_groups={{0,1,16,17,32,33,48,49},{2,3,18,19,34,35,50,51},{4,5,20,21,36,37,52,53}..., dimensions={0} | all-to-all | bytes 3964928 | tf_op jit(solution)/shard_map/cond/branch_1_fun/all_to_all | solution.py:344
  53.8 1.5 %cut.1 = (bf16[1544,128]{1,0:T(8,128)(2,1)}, bf16[1544,128]{1,0:T(8,128)(2,1)}, bf16[1544,128]{1,0:T(8,128)(2,1)}, bf16[1544,128]{1,0:T(8,128)(2,1)}, bf16[1544,128]{1,0:T(8,128)(2,1)}) custom-call(bf16[8,968,128]{2,1,0:T(8,128)(2,1)S(1)} %all_to_all.20.got_ref), custom_call_target="tpu_custom_call" | custom-call | tf_op jit(solution)/shard_map/cond/branch_1_fun/cut/pallas_call | solution.py:401
  55.3 1.4 %collective-permute-start.3 = (bf16[1544,128]{1,0:T(8,128)(2,1)}, bf16[1544,128]{1,0:T(8,128)(2,1)S(1)}, u32[]{:S(2)}, u32[]{:S(2)}) collective-permute-start(bf16[1544,128]{1,0:T(8,128)(2,1)} %get-tuple-element.39), channel_id=1, source_target_pairs={{0,4},{1,5},{2,6},{3,7},{4,8},{5,9},{6,10},{7,11},{8,12},{9,13},{1... | collective-permute-start | bytes 1185800 | tf_op jit(solution)/shard_map/ppermute | solution.py:338
  56.6 2.2 %collective-permute-start.4 = (bf16[1544,128]{1,0:T(8,128)(2,1)}, bf16[1544,128]{1,0:T(8,128)(2,1)S(1)}, u32[]{:S(2)}, u32[]{:S(2)}) collective-permute-start(bf16[1544,128]{1,0:T(8,128)(2,1)} %get-tuple-element.40), channel_id=1, source_target_pairs={{0,12},{1,13},{2,14},{3,15},{4,0},{5,1},{6,2},{7,3},{8,4},{9,5},{1... | collective-permute-start | bytes 1185800 | tf_op jit(solution)/shard_map/ppermute | solution.py:338
  58.8 0.0 collective-permute-done
  58.9 0.9 collective-permute-start.5
  59.7 0.0 collective-permute-done.1
  59.8 1.8 %collective-permute-start.6 = (bf16[1544,128]{1,0:T(8,128)(2,1)}, bf16[1544,128]{1,0:T(8,128)(2,1)S(1)}, u32[]{:S(2)}, u32[]{:S(2)}) collective-permute-start(bf16[1544,128]{1,0:T(8,128)(2,1)} %get-tuple-element.43), channel_id=1, source_target_pairs={{0,14},{1,15},{2,0},{3,1},{4,2},{5,3},{6,4},{7,5},{8,6},{9,7},{10,... | collective-permute-start | bytes 1185800 | tf_op jit(solution)/shard_map/ppermute | solution.py:338
  61.5 0.0 collective-permute-done.2
  61.5 22.3 %conditional.2 = (bf16[8,584,128]{2,1,0:T(8,128)(2,1)S(1)}) conditional(s32[]{:T(128)} %bitcast.2, () %tuple.18, (bf16[1544,128]{1,0:T(8,128)(2,1)}, bf16[1544,128]{1,0:T(8,128)(2,1)}, bf16[1544,128]{1,0:T(8,128)(2,1)}) %tuple.19), branch_computations={%region_0.0_spmd, %region_1.0_spmd} | conditional | bytes 2392072 | solution.py:350
  61.5 1.4 %merge.1 = bf16[8,584,128]{2,1,0:T(8,128)(2,1)S(1)} custom-call(bf16[1544,128]{1,0:T(8,128)(2,1)} %get-tuple-element.15.refs_0_, bf16[1544,128]{1,0:T(8,128)(2,1)} %get-tuple-element.16.refs_1_, bf16[1544,128]{1,0:T(8,128)(2,1)} %get-tuple-element.17.refs_2_), custom_call_target="tpu_custom_call" | custom-call | tf_op jit(solution)/shard_map/cond/branch_1_fun/merge/pallas_call | solution.py:410
  62.9 21.0 %all_to_all.19 = bf16[8,584,128]{2,1,0:T(8,128)(2,1)S(1)} all-to-all(bf16[8,584,128]{2,1,0:T(8,128)(2,1)S(1)} %merge.1), channel_id=1, replica_groups={{0,1,16,17,32,33,48,49},{2,3,18,19,34,35,50,51},{4,5,20,21,36,37,52,53}..., dimensions={0} | all-to-all | bytes 2392064 | tf_op jit(solution)/shard_map/cond/branch_1_fun/all_to_all | solution.py:344
  83.9 0.0 collective-permute-done.3.refs_0_
  83.9 3.4 %best_early.1.refs_5_ = f32[8,1536]{1,0:T(8,128)S(1)} custom-call(bf16[8,584,128]{2,1,0:T(8,128)(2,1)S(1)} %get-tuple-element.54.early_hbm, bf16[1544,128]{1,0:T(8,128)(2,1)S(1)} %collective-permute-done.3.refs_0_, bf16[1544,128]{1,0:T(8,128)(2,1)S(1)} %collective-permute-done.4.refs_1_, bf16[1544,128]{1,0:T(8,128)(2,1)S(1)} %copy-done), custom_call_target="tpu_custom_call" | custom-call | flops 1811939328 | bytes 8388608 | tf_op jit(solution)/shard_map/best_early/pallas_call | solution.py:424
  87.3 0.0 collective-permute-done.6.refs_4_
  87.4 3.2 %best_last.1 = f32[64,32]{1,0:T(8,128)S(1)} custom-call(bf16[8,584,128]{2,1,0:T(8,128)(2,1)S(1)} %get-tuple-element.54.early_hbm, bf16[1544,128]{1,0:T(8,128)(2,1)S(1)} %collective-permute-done.3.refs_0_, bf16[1544,128]{1,0:T(8,128)(2,1)S(1)} %collective-permute-done.4.refs_1_, bf16[1544,128]{1,0:T(8,128)(2,1)S(1)} %copy-done, ...), custom_call_target="tpu_custom_call" | custom-call | flops 3221225472 | bytes 8388608 | tf_op jit(solution)/shard_map/best_last/pallas_call | solution.py:424
  90.6 13.5 %all_to_all.21 = f32[64,1,32]{2,1,0:T(1,128)S(1)} all-to-all(f32[64,1,32]{2,1,0:T(1,128)S(1)} %bitcast.9), channel_id=1, replica_groups=mesh['outer'=4,'member'=64] {'member'}, dimensions={0} | all-to-all | bytes 16384 | tf_op jit(solution)/shard_map/all_to_all | solution.py:443
  104.1 1.0 home.1
  (4 shorter events, 0.0 us)
Async XLA Ops:
  3.2 55.7 %collective-permute-start = (bf16[1544,128]{1,0:T(8,128)(2,1)S(1)}, bf16[1544,128]{1,0:T(8,128)(2,1)}, u32[]{:S(2)}, u32[]{:S(2)}) collective-permute-start(bf16[1544,128]{1,0:T(8,128)(2,1)S(1)} %get-tuple-element.32), channel_id=1, source_target_pairs={{0,8},{1,9},{2,10},{3,11},{4,12},{5,13},{6,14},{7,15},{8,0},{9,1},... | collective-permute-start | bytes 1185800 | tf_op jit(solution)/shard_map/ppermute | solution.py:338
  17.2 42.5 %collective-permute-start.1 = (bf16[1544,128]{1,0:T(8,128)(2,1)S(1)}, bf16[1544,128]{1,0:T(8,128)(2,1)}, u32[]{:S(2)}, u32[]{:S(2)}) collective-permute-start(bf16[1544,128]{1,0:T(8,128)(2,1)S(1)} %get-tuple-element.36), channel_id=1, source_target_pairs={{0,6},{1,7},{2,8},{3,9},{4,10},{5,11},{6,12},{7,13},{8,14},{9,15},... | collective-permute-start | bytes 1185800 | tf_op jit(solution)/shard_map/ppermute | solution.py:338
  18.9 42.6 %collective-permute-start.2 = (bf16[1544,128]{1,0:T(8,128)(2,1)S(1)}, bf16[1544,128]{1,0:T(8,128)(2,1)}, u32[]{:S(2)}, u32[]{:S(2)}) collective-permute-start(bf16[1544,128]{1,0:T(8,128)(2,1)S(1)} %get-tuple-element.37), channel_id=1, source_target_pairs={{0,10},{1,11},{2,12},{3,13},{4,14},{5,15},{6,0},{7,1},{8,2},{9,3},... | collective-permute-start | bytes 1185800 | tf_op jit(solution)/shard_map/ppermute | solution.py:338
  55.3 28.6 %collective-permute-start.3 = (bf16[1544,128]{1,0:T(8,128)(2,1)}, bf16[1544,128]{1,0:T(8,128)(2,1)S(1)}, u32[]{:S(2)}, u32[]{:S(2)}) collective-permute-start(bf16[1544,128]{1,0:T(8,128)(2,1)} %get-tuple-element.39), channel_id=1, source_target_pairs={{0,4},{1,5},{2,6},{3,7},{4,8},{5,9},{6,10},{7,11},{8,12},{9,13},{1... | collective-permute-start | bytes 1185800 | tf_op jit(solution)/shard_map/ppermute | solution.py:338
  56.6 27.2 %collective-permute-start.4 = (bf16[1544,128]{1,0:T(8,128)(2,1)}, bf16[1544,128]{1,0:T(8,128)(2,1)S(1)}, u32[]{:S(2)}, u32[]{:S(2)}) collective-permute-start(bf16[1544,128]{1,0:T(8,128)(2,1)} %get-tuple-element.40), channel_id=1, source_target_pairs={{0,12},{1,13},{2,14},{3,15},{4,0},{5,1},{6,2},{7,3},{8,4},{9,5},{1... | collective-permute-start | bytes 1185800 | tf_op jit(solution)/shard_map/ppermute | solution.py:338
  58.9 28.5 %collective-permute-start.5 = (bf16[1544,128]{1,0:T(8,128)(2,1)}, bf16[1544,128]{1,0:T(8,128)(2,1)S(1)}, u32[]{:S(2)}, u32[]{:S(2)}) collective-permute-start(bf16[1544,128]{1,0:T(8,128)(2,1)} %get-tuple-element.42), channel_id=1, source_target_pairs={{0,2},{1,3},{2,4},{3,5},{4,6},{5,7},{6,8},{7,9},{8,10},{9,11},{10,... | collective-permute-start | bytes 1185800 | tf_op jit(solution)/shard_map/ppermute | solution.py:338
  59.8 27.6 %collective-permute-start.6 = (bf16[1544,128]{1,0:T(8,128)(2,1)}, bf16[1544,128]{1,0:T(8,128)(2,1)S(1)}, u32[]{:S(2)}, u32[]{:S(2)}) collective-permute-start(bf16[1544,128]{1,0:T(8,128)(2,1)} %get-tuple-element.43), channel_id=1, source_target_pairs={{0,14},{1,15},{2,0},{3,1},{4,2},{5,3},{6,4},{7,5},{8,6},{9,7},{10,... | collective-permute-start | bytes 1185800 | tf_op jit(solution)/shard_map/ppermute | solution.py:338
  61.5 22.3 %copy-start = (bf16[1544,128]{1,0:T(8,128)(2,1)S(1)}, bf16[1544,128]{1,0:T(8,128)(2,1)}, u32[]{:S(2)}) copy-start(bf16[1544,128]{1,0:T(8,128)(2,1)} %get-tuple-element.41.refs_2_) | copy-start | bytes 1185796

commit v6 on v5

--- a/solution.py
+++ b/solution.py
@@ -31,6 +31,14 @@
 
 def dot_t(a, b):
     return lax.dot_general(a, b, (((1,), (1,)), ((), ())), preferred_element_type=F32)
+
+
+def bf16_parts(x):
+    parts = []
+    for _ in range(3):
+        parts.append(x.astype(BF16))
+        x = x - parts[-1].astype(F32)
+    return parts
 
 
 def wide_row(ref):
@@ -282,13 +290,10 @@
             to = (iota((out_ref.shape[0], TILE), 0) == home).astype(BF16)
             own = iota((per_pair, TILE), 0) == place_in % per_pair
             rest = jnp.where(own, jnp.concatenate(parts, axis=1), 0.0)
-            for _ in range(3):
-                piece = rest.astype(BF16)
-                rest = rest - piece.astype(F32)
-                add = dot_t(to, piece)
-                total = add if total is None else total + add
+            add = dot_t(to, jnp.concatenate(bf16_parts(rest), axis=0))
+            total = add if total is None else total + add
     if last:
-        out_ref[...] = total
+        out_ref[...] = sum(total[:, n * per_pair : (n + 1) * per_pair] for n in range(3))
 
 
 def home_kernel(ret_ref, pos_ref, out_ref):
@@ -298,12 +303,7 @@
     owner = pos // per_pair
     rank = pos - owner * per_pair
     slot = (iota((per_pair, rows), 0) == rank).astype(BF16)
-    rest = ret_ref[...]
-    spread = jnp.zeros((owners, rows), F32)
-    for _ in range(3):
-        part = rest.astype(BF16)
-        rest = rest - part.astype(F32)
-        spread = spread + dot(part, slot)
+    spread = dot(jnp.concatenate(bf16_parts(ret_ref[...]), axis=1), jnp.concatenate([slot] * 3, axis=0))
     mine = jnp.where(iota((owners, rows), 0) == owner, spread, 0.0)
     put_row(out_ref, jnp.sum(mine, axis=0, keepdims=True))
 

time: 105 us -> 105 us (level)
  no operation moved by 1% of the time
where the time goes in v6:
time: 105 us
  blocking collectives  65.8 us (63%)
  Pallas kernels  19.7 us (19%)
  starting transfers between devices  18.6 us (18%)
    all_to_all x2, blocking collectives, in_plane(): lax.all_to_all(rows, 'member', split_axis=0, concat_axis=0, tiled=True, a...  52.3 us
    ppermute x7, starting transfers between devices, to_shift(): return lax.ppermute(rows, 'member', pairs)  18.6 us
    all_to_all x1, blocking collectives, on_device(): lax.all_to_all(best, 'member', split_axis=0, concat_axis=0, tiled=True)  13.5 us
    pallas_call x2, Pallas kernels, best_of(): pl.pallas_call(functools.partial(best_kernel, per_pair, last), in_specs=[...  6.59 us
    pallas_call x1, Pallas kernels, on_device(): send(rest_kernel, NEXT, [shape((PLANE, len(LATE) * tall + META, LANES), B...  6.18 us
    pallas_call x1, Pallas kernels, on_device(): pl.pallas_call(functools.partial(first_kernel, members, per_owner, per_pa...  3.19 us
  transfers between devices with their start and end apart: 7, of which 0 were waited for; matrix products, arithmetic and copies ran while one was open for 0% of the time, Pallas kernels for 12%

profile of v6, /device:TPU:1, one launch (start us, length us, event | category | flops | bytes accessed | tf_op | source)
XLA Modules:
  0.0 104.9 jit_solution(679822633299737053)
XLA Ops:
  0.0 3.2 %send_first.1 = (bf16[1544,128]{1,0:T(8,128)(2,1)S(1)}, s32[16,128]{1,0:T(8,128)S(1)}, f32[64,128]{1,0:T(8,128)S(1)}, s32[1]{0:T(128)}, bf16[2048,768]{1,0:T(8,128)(2,1)S(1)}) custom-call(s32[16,128]{1,0:T(8,128)} %bitcast.10, s32[16,128]{1,0:T(8,128)} %bitcast.11, bf16[2048,768]{1,0:T(8,128)(2,1)} %emb_hbm.1), custom_call_target="tpu_custom_call" | custom-call | flops 805306368 | bytes 8388608 | tf_op jit(solution)/shard_map/send_first/pallas_call | solution.py:361
  3.2 7.8 %collective-permute-start = (bf16[1544,128]{1,0:T(8,128)(2,1)S(1)}, bf16[1544,128]{1,0:T(8,128)(2,1)}, u32[]{:S(2)}, u32[]{:S(2)}) collective-permute-start(bf16[1544,128]{1,0:T(8,128)(2,1)S(1)} %get-tuple-element.32), channel_id=1, source_target_pairs={{0,8},{1,9},{2,10},{3,11},{4,12},{5,13},{6,14},{7,15},{8,0},{9,1},... | collective-permute-start | bytes 1185800 | tf_op jit(solution)/shard_map/ppermute | solution.py:338
  11.0 6.2 %send_rest.1 = (bf16[1544,128]{1,0:T(8,128)(2,1)S(1)}, bf16[1544,128]{1,0:T(8,128)(2,1)S(1)}, bf16[8,968,128]{2,1,0:T(8,128)(2,1)S(1)}) custom-call(s32[16,128]{1,0:T(8,128)S(1)} %get-tuple-element.33.pos_ref, f32[64,128]{1,0:T(8,128)S(1)} %get-tuple-element.34.meta_ref, bf16[2048,768]{1,0:T(8,128)(2,1)S(1)} %get-tuple-element.35.emb_ref), custom_call_target="tpu_custom_call" | custom-call | flops 1610612736 | bytes 8388608 | tf_op jit(solution)/shard_map/send_rest/pallas_call | solution.py:394
  17.2 1.7 %collective-permute-start.1 = (bf16[1544,128]{1,0:T(8,128)(2,1)S(1)}, bf16[1544,128]{1,0:T(8,128)(2,1)}, u32[]{:S(2)}, u32[]{:S(2)}) collective-permute-start(bf16[1544,128]{1,0:T(8,128)(2,1)S(1)} %get-tuple-element.36), channel_id=1, source_target_pairs={{0,6},{1,7},{2,8},{3,9},{4,10},{5,11},{6,12},{7,13},{8,14},{9,15},... | collective-permute-start | bytes 1185800 | tf_op jit(solution)/shard_map/ppermute | solution.py:338
  18.9 2.8 %collective-permute-start.2 = (bf16[1544,128]{1,0:T(8,128)(2,1)S(1)}, bf16[1544,128]{1,0:T(8,128)(2,1)}, u32[]{:S(2)}, u32[]{:S(2)}) collective-permute-start(bf16[1544,128]{1,0:T(8,128)(2,1)S(1)} %get-tuple-element.37), channel_id=1, source_target_pairs={{0,10},{1,11},{2,12},{3,13},{4,14},{5,15},{6,0},{7,1},{8,2},{9,3},... | collective-permute-start | bytes 1185800 | tf_op jit(solution)/shard_map/ppermute | solution.py:338
  22.4 32.9 %conditional.3 = ((bf16[1544,128]{1,0:T(8,128)(2,1)}, bf16[1544,128]{1,0:T(8,128)(2,1)}, bf16[1544,128]{1,0:T(8,128)(2,1)}, bf16[1544,128]{1,0:T(8,128)(2,1)}, bf16[1544,128]{1,0:T(8,128)(2,1)})) conditional(s32[]{:T(128)} %bitcast.2, () %tuple.20, bf16[8,968,128]{2,1,0:T(8,128)(2,1)S(1)} %get-tuple-element.38), branch_computations={%region_2.0_spmd, %region_3.0_spmd} | conditional | bytes 3964936 | solution.py:350
  22.4 31.4 %all_to_all.20.got_ref = bf16[8,968,128]{2,1,0:T(8,128)(2,1)S(1)} all-to-all(bf16[8,968,128]{2,1,0:T(8,128)(2,1)S(1)} %param.3), channel_id=1, replica_groups={{0,1,16,17,32,33,48,49},{2,3,18,19,34,35,50,51},{4,5,20,21,36,37,52,53}..., dimensions={0} | all-to-all | bytes 3964928 | tf_op jit(solution)/shard_map/cond/branch_1_fun/all_to_all | solution.py:344
  53.8 1.5 %cut.1 = (bf16[1544,128]{1,0:T(8,128)(2,1)}, bf16[1544,128]{1,0:T(8,128)(2,1)}, bf16[1544,128]{1,0:T(8,128)(2,1)}, bf16[1544,128]{1,0:T(8,128)(2,1)}, bf16[1544,128]{1,0:T(8,128)(2,1)}) custom-call(bf16[8,968,128]{2,1,0:T(8,128)(2,1)S(1)} %all_to_all.20.got_ref), custom_call_target="tpu_custom_call" | custom-call | tf_op jit(solution)/shard_map/cond/branch_1_fun/cut/pallas_call | solution.py:401
  55.3 1.4 %collective-permute-start.3 = (bf16[1544,128]{1,0:T(8,128)(2,1)}, bf16[1544,128]{1,0:T(8,128)(2,1)S(1)}, u32[]{:S(2)}, u32[]{:S(2)}) collective-permute-start(bf16[1544,128]{1,0:T(8,128)(2,1)} %get-tuple-element.39), channel_id=1, source_target_pairs={{0,4},{1,5},{2,6},{3,7},{4,8},{5,9},{6,10},{7,11},{8,12},{9,13},{1... | collective-permute-start | bytes 1185800 | tf_op jit(solution)/shard_map/ppermute | solution.py:338
  56.6 2.2 %collective-permute-start.4 = (bf16[1544,128]{1,0:T(8,128)(2,1)}, bf16[1544,128]{1,0:T(8,128)(2,1)S(1)}, u32[]{:S(2)}, u32[]{:S(2)}) collective-permute-start(bf16[1544,128]{1,0:T(8,128)(2,1)} %get-tuple-element.40), channel_id=1, source_target_pairs={{0,12},{1,13},{2,14},{3,15},{4,0},{5,1},{6,2},{7,3},{8,4},{9,5},{1... | collective-permute-start | bytes 1185800 | tf_op jit(solution)/shard_map/ppermute | solution.py:338
  58.8 0.0 collective-permute-done
  58.9 0.9 collective-permute-start.5
  59.8 1.8 %collective-permute-start.6 = (bf16[1544,128]{1,0:T(8,128)(2,1)}, bf16[1544,128]{1,0:T(8,128)(2,1)S(1)}, u32[]{:S(2)}, u32[]{:S(2)}) collective-permute-start(bf16[1544,128]{1,0:T(8,128)(2,1)} %get-tuple-element.43), channel_id=1, source_target_pairs={{0,14},{1,15},{2,0},{3,1},{4,2},{5,3},{6,4},{7,5},{8,6},{9,7},{10,... | collective-permute-start | bytes 1185800 | tf_op jit(solution)/shard_map/ppermute | solution.py:338
  61.5 0.0 collective-permute-done.2
  61.5 22.3 %conditional.2 = (bf16[8,584,128]{2,1,0:T(8,128)(2,1)S(1)}) conditional(s32[]{:T(128)} %bitcast.2, () %tuple.18, (bf16[1544,128]{1,0:T(8,128)(2,1)}, bf16[1544,128]{1,0:T(8,128)(2,1)}, bf16[1544,128]{1,0:T(8,128)(2,1)}) %tuple.19), branch_computations={%region_0.0_spmd, %region_1.0_spmd} | conditional | bytes 2392072 | solution.py:350
  61.5 1.4 %merge.1 = bf16[8,584,128]{2,1,0:T(8,128)(2,1)S(1)} custom-call(bf16[1544,128]{1,0:T(8,128)(2,1)} %get-tuple-element.15.refs_0_, bf16[1544,128]{1,0:T(8,128)(2,1)} %get-tuple-element.16.refs_1_, bf16[1544,128]{1,0:T(8,128)(2,1)} %get-tuple-element.17.refs_2_), custom_call_target="tpu_custom_call" | custom-call | tf_op jit(solution)/shard_map/cond/branch_1_fun/merge/pallas_call | solution.py:410
  62.9 21.0 %all_to_all.19 = bf16[8,584,128]{2,1,0:T(8,128)(2,1)S(1)} all-to-all(bf16[8,584,128]{2,1,0:T(8,128)(2,1)S(1)} %merge.1), channel_id=1, replica_groups={{0,1,16,17,32,33,48,49},{2,3,18,19,34,35,50,51},{4,5,20,21,36,37,52,53}..., dimensions={0} | all-to-all | bytes 2392064 | tf_op jit(solution)/shard_map/cond/branch_1_fun/all_to_all | solution.py:344
  83.9 0.0 collective-permute-done.3.refs_0_
  83.9 0.0 collective-permute-done.4.refs_1_
  83.9 3.4 %best_early.1.refs_5_ = f32[8,1536]{1,0:T(8,128)S(1)} custom-call(bf16[8,584,128]{2,1,0:T(8,128)(2,1)S(1)} %get-tuple-element.54.early_hbm, bf16[1544,128]{1,0:T(8,128)(2,1)S(1)} %collective-permute-done.3.refs_0_, bf16[1544,128]{1,0:T(8,128)(2,1)S(1)} %collective-permute-done.4.refs_1_, bf16[1544,128]{1,0:T(8,128)(2,1)S(1)} %copy-done), custom_call_target="tpu_custom_call" | custom-call | flops 1811939328 | bytes 8388608 | tf_op jit(solution)/shard_map/best_early/pallas_call | solution.py:424
  87.3 0.0 collective-permute-done.6.refs_4_
  87.4 3.1 %best_last.1 = f32[64,32]{1,0:T(8,128)S(1)} custom-call(bf16[8,584,128]{2,1,0:T(8,128)(2,1)S(1)} %get-tuple-element.54.early_hbm, bf16[1544,128]{1,0:T(8,128)(2,1)S(1)} %collective-permute-done.3.refs_0_, bf16[1544,128]{1,0:T(8,128)(2,1)S(1)} %collective-permute-done.4.refs_1_, bf16[1544,128]{1,0:T(8,128)(2,1)S(1)} %copy-done, ...), custom_call_target="tpu_custom_call" | custom-call | flops 3221225472 | bytes 8388608 | tf_op jit(solution)/shard_map/best_last/pallas_call | solution.py:424
  90.5 13.5 %all_to_all.21 = f32[64,1,32]{2,1,0:T(1,128)S(1)} all-to-all(f32[64,1,32]{2,1,0:T(1,128)S(1)} %bitcast.9), channel_id=1, replica_groups=mesh['outer'=4,'member'=64] {'member'}, dimensions={0} | all-to-all | bytes 16384 | tf_op jit(solution)/shard_map/all_to_all | solution.py:443
  104.0 0.9 home.1
  (4 shorter events, 0.0 us)
Async XLA Ops:
  3.2 55.7 %collective-permute-start = (bf16[1544,128]{1,0:T(8,128)(2,1)S(1)}, bf16[1544,128]{1,0:T(8,128)(2,1)}, u32[]{:S(2)}, u32[]{:S(2)}) collective-permute-start(bf16[1544,128]{1,0:T(8,128)(2,1)S(1)} %get-tuple-element.32), channel_id=1, source_target_pairs={{0,8},{1,9},{2,10},{3,11},{4,12},{5,13},{6,14},{7,15},{8,0},{9,1},... | collective-permute-start | bytes 1185800 | tf_op jit(solution)/shard_map/ppermute | solution.py:338
  17.2 42.5 %collective-permute-start.1 = (bf16[1544,128]{1,0:T(8,128)(2,1)S(1)}, bf16[1544,128]{1,0:T(8,128)(2,1)}, u32[]{:S(2)}, u32[]{:S(2)}) collective-permute-start(bf16[1544,128]{1,0:T(8,128)(2,1)S(1)} %get-tuple-element.36), channel_id=1, source_target_pairs={{0,6},{1,7},{2,8},{3,9},{4,10},{5,11},{6,12},{7,13},{8,14},{9,15},... | collective-permute-start | bytes 1185800 | tf_op jit(solution)/shard_map/ppermute | solution.py:338
  18.9 42.6 %collective-permute-start.2 = (bf16[1544,128]{1,0:T(8,128)(2,1)S(1)}, bf16[1544,128]{1,0:T(8,128)(2,1)}, u32[]{:S(2)}, u32[]{:S(2)}) collective-permute-start(bf16[1544,128]{1,0:T(8,128)(2,1)S(1)} %get-tuple-element.37), channel_id=1, source_target_pairs={{0,10},{1,11},{2,12},{3,13},{4,14},{5,15},{6,0},{7,1},{8,2},{9,3},... | collective-permute-start | bytes 1185800 | tf_op jit(solution)/shard_map/ppermute | solution.py:338
  55.3 28.6 %collective-permute-start.3 = (bf16[1544,128]{1,0:T(8,128)(2,1)}, bf16[1544,128]{1,0:T(8,128)(2,1)S(1)}, u32[]{:S(2)}, u32[]{:S(2)}) collective-permute-start(bf16[1544,128]{1,0:T(8,128)(2,1)} %get-tuple-element.39), channel_id=1, source_target_pairs={{0,4},{1,5},{2,6},{3,7},{4,8},{5,9},{6,10},{7,11},{8,12},{9,13},{1... | collective-permute-start | bytes 1185800 | tf_op jit(solution)/shard_map/ppermute | solution.py:338
  56.6 27.2 %collective-permute-start.4 = (bf16[1544,128]{1,0:T(8,128)(2,1)}, bf16[1544,128]{1,0:T(8,128)(2,1)S(1)}, u32[]{:S(2)}, u32[]{:S(2)}) collective-permute-start(bf16[1544,128]{1,0:T(8,128)(2,1)} %get-tuple-element.40), channel_id=1, source_target_pairs={{0,12},{1,13},{2,14},{3,15},{4,0},{5,1},{6,2},{7,3},{8,4},{9,5},{1... | collective-permute-start | bytes 1185800 | tf_op jit(solution)/shard_map/ppermute | solution.py:338
  58.9 28.5 %collective-permute-start.5 = (bf16[1544,128]{1,0:T(8,128)(2,1)}, bf16[1544,128]{1,0:T(8,128)(2,1)S(1)}, u32[]{:S(2)}, u32[]{:S(2)}) collective-permute-start(bf16[1544,128]{1,0:T(8,128)(2,1)} %get-tuple-element.42), channel_id=1, source_target_pairs={{0,2},{1,3},{2,4},{3,5},{4,6},{5,7},{6,8},{7,9},{8,10},{9,11},{10,... | collective-permute-start | bytes 1185800 | tf_op jit(solution)/shard_map/ppermute | solution.py:338
  59.8 27.6 %collective-permute-start.6 = (bf16[1544,128]{1,0:T(8,128)(2,1)}, bf16[1544,128]{1,0:T(8,128)(2,1)S(1)}, u32[]{:S(2)}, u32[]{:S(2)}) collective-permute-start(bf16[1544,128]{1,0:T(8,128)(2,1)} %get-tuple-element.43), channel_id=1, source_target_pairs={{0,14},{1,15},{2,0},{3,1},{4,2},{5,3},{6,4},{7,5},{8,6},{9,7},{10,... | collective-permute-start | bytes 1185800 | tf_op jit(solution)/shard_map/ppermute | solution.py:338
  61.5 22.3 %copy-start = (bf16[1544,128]{1,0:T(8,128)(2,1)S(1)}, bf16[1544,128]{1,0:T(8,128)(2,1)}, u32[]{:S(2)}) copy-start(bf16[1544,128]{1,0:T(8,128)(2,1)} %get-tuple-element.41.refs_2_) | copy-start | bytes 1185796

commit v7 on v5

--- a/solution.py
+++ b/solution.py
@@ -154,7 +154,7 @@
     goal = place(wide_row(pos_ref), per_pair, LATE, True)
     some = len(LATE) * per_pair
     tall = emb_ref.shape[1] // LANES * per_pair
-    step = 4
+    step = 8
     for p0 in range(0, PLANE, step):
         unit = scaled(dot(picked(goal, p0 * some, step * some), emb_ref[...]))
         for p in range(p0, p0 + step):

time: 105 us -> 106 us (level)
  no operation moved by 1% of the time
where the time goes in v7:
time: 106 us; the launch traced here: 105 us
  blocking collectives  65.9 us (62%)
  Pallas kernels  20.1 us (19%)
  starting transfers between devices  18.6 us (18%)
    all_to_all x2, blocking collectives, in_plane(): lax.all_to_all(rows, 'member', split_axis=0, concat_axis=0, tiled=True, a...  52.3 us
    ppermute x7, starting transfers between devices, to_shift(): return lax.ppermute(rows, 'member', pairs)  18.6 us
    all_to_all x1, blocking collectives, on_device(): lax.all_to_all(best, 'member', split_axis=0, concat_axis=0, tiled=True)  13.5 us
    pallas_call x2, Pallas kernels, best_of(): pl.pallas_call(functools.partial(best_kernel, per_pair, last), in_specs=[...  6.67 us
    pallas_call x1, Pallas kernels, on_device(): send(rest_kernel, NEXT, [shape((PLANE, len(LATE) * tall + META, LANES), B...  6.43 us
    pallas_call x1, Pallas kernels, on_device(): pl.pallas_call(functools.partial(first_kernel, members, per_owner, per_pa...  3.19 us
  transfers between devices with their start and end apart: 7, of which 0 were waited for; matrix products, arithmetic and copies ran while one was open for 0% of the time, Pallas kernels for 12%

profile of v7, /device:TPU:1, one launch (start us, length us, event | category | flops | bytes accessed | tf_op | source)
XLA Modules:
  0.0 105.3 jit_solution(13007529785197161085)
XLA Ops:
  0.0 3.2 %send_first.1 = (bf16[1544,128]{1,0:T(8,128)(2,1)S(1)}, s32[16,128]{1,0:T(8,128)S(1)}, f32[64,128]{1,0:T(8,128)S(1)}, s32[1]{0:T(128)}, bf16[2048,768]{1,0:T(8,128)(2,1)S(1)}) custom-call(s32[16,128]{1,0:T(8,128)} %bitcast.10, s32[16,128]{1,0:T(8,128)} %bitcast.11, bf16[2048,768]{1,0:T(8,128)(2,1)} %emb_hbm.1), custom_call_target="tpu_custom_call" | custom-call | flops 805306368 | bytes 8388608 | tf_op jit(solution)/shard_map/send_first/pallas_call | solution.py:361
  3.2 7.8 %collective-permute-start = (bf16[1544,128]{1,0:T(8,128)(2,1)S(1)}, bf16[1544,128]{1,0:T(8,128)(2,1)}, u32[]{:S(2)}, u32[]{:S(2)}) collective-permute-start(bf16[1544,128]{1,0:T(8,128)(2,1)S(1)} %get-tuple-element.32), channel_id=1, source_target_pairs={{0,8},{1,9},{2,10},{3,11},{4,12},{5,13},{6,14},{7,15},{8,0},{9,1},... | collective-permute-start | bytes 1185800 | tf_op jit(solution)/shard_map/ppermute | solution.py:338
  11.0 6.4 %send_rest.1 = (bf16[1544,128]{1,0:T(8,128)(2,1)S(1)}, bf16[1544,128]{1,0:T(8,128)(2,1)S(1)}, bf16[8,968,128]{2,1,0:T(8,128)(2,1)S(1)}) custom-call(s32[16,128]{1,0:T(8,128)S(1)} %get-tuple-element.33.pos_ref, f32[64,128]{1,0:T(8,128)S(1)} %get-tuple-element.34.meta_ref, bf16[2048,768]{1,0:T(8,128)(2,1)S(1)} %get-tuple-element.35.emb_ref), custom_call_target="tpu_custom_call" | custom-call | flops 1610612736 | bytes 8388608 | tf_op jit(solution)/shard_map/send_rest/pallas_call | solution.py:394
  17.5 1.7 %collective-permute-start.1 = (bf16[1544,128]{1,0:T(8,128)(2,1)S(1)}, bf16[1544,128]{1,0:T(8,128)(2,1)}, u32[]{:S(2)}, u32[]{:S(2)}) collective-permute-start(bf16[1544,128]{1,0:T(8,128)(2,1)S(1)} %get-tuple-element.36), channel_id=1, source_target_pairs={{0,6},{1,7},{2,8},{3,9},{4,10},{5,11},{6,12},{7,13},{8,14},{9,15},... | collective-permute-start | bytes 1185800 | tf_op jit(solution)/shard_map/ppermute | solution.py:338
  19.2 2.8 %collective-permute-start.2 = (bf16[1544,128]{1,0:T(8,128)(2,1)S(1)}, bf16[1544,128]{1,0:T(8,128)(2,1)}, u32[]{:S(2)}, u32[]{:S(2)}) collective-permute-start(bf16[1544,128]{1,0:T(8,128)(2,1)S(1)} %get-tuple-element.37), channel_id=1, source_target_pairs={{0,10},{1,11},{2,12},{3,13},{4,14},{5,15},{6,0},{7,1},{8,2},{9,3},... | collective-permute-start | bytes 1185800 | tf_op jit(solution)/shard_map/ppermute | solution.py:338
  22.7 32.9 %conditional.3 = ((bf16[1544,128]{1,0:T(8,128)(2,1)}, bf16[1544,128]{1,0:T(8,128)(2,1)}, bf16[1544,128]{1,0:T(8,128)(2,1)}, bf16[1544,128]{1,0:T(8,128)(2,1)}, bf16[1544,128]{1,0:T(8,128)(2,1)})) conditional(s32[]{:T(128)} %bitcast.2, () %tuple.20, bf16[8,968,128]{2,1,0:T(8,128)(2,1)S(1)} %get-tuple-element.38), branch_computations={%region_2.0_spmd, %region_3.0_spmd} | conditional | bytes 3964936 | solution.py:350
  22.7 31.4 %all_to_all.20.got_ref = bf16[8,968,128]{2,1,0:T(8,128)(2,1)S(1)} all-to-all(bf16[8,968,128]{2,1,0:T(8,128)(2,1)S(1)} %param.3), channel_id=1, replica_groups={{0,1,16,17,32,33,48,49},{2,3,18,19,34,35,50,51},{4,5,20,21,36,37,52,53}..., dimensions={0} | all-to-all | bytes 3964928 | tf_op jit(solution)/shard_map/cond/branch_1_fun/all_to_all | solution.py:344
  54.1 1.5 %cut.1 = (bf16[1544,128]{1,0:T(8,128)(2,1)}, bf16[1544,128]{1,0:T(8,128)(2,1)}, bf16[1544,128]{1,0:T(8,128)(2,1)}, bf16[1544,128]{1,0:T(8,128)(2,1)}, bf16[1544,128]{1,0:T(8,128)(2,1)}) custom-call(bf16[8,968,128]{2,1,0:T(8,128)(2,1)S(1)} %all_to_all.20.got_ref), custom_call_target="tpu_custom_call" | custom-call | tf_op jit(solution)/shard_map/cond/branch_1_fun/cut/pallas_call | solution.py:401
  55.5 1.4 %collective-permute-start.3 = (bf16[1544,128]{1,0:T(8,128)(2,1)}, bf16[1544,128]{1,0:T(8,128)(2,1)S(1)}, u32[]{:S(2)}, u32[]{:S(2)}) collective-permute-start(bf16[1544,128]{1,0:T(8,128)(2,1)} %get-tuple-element.39), channel_id=1, source_target_pairs={{0,4},{1,5},{2,6},{3,7},{4,8},{5,9},{6,10},{7,11},{8,12},{9,13},{1... | collective-permute-start | bytes 1185800 | tf_op jit(solution)/shard_map/ppermute | solution.py:338
  56.9 2.2 %collective-permute-start.4 = (bf16[1544,128]{1,0:T(8,128)(2,1)}, bf16[1544,128]{1,0:T(8,128)(2,1)S(1)}, u32[]{:S(2)}, u32[]{:S(2)}) collective-permute-start(bf16[1544,128]{1,0:T(8,128)(2,1)} %get-tuple-element.40), channel_id=1, source_target_pairs={{0,12},{1,13},{2,14},{3,15},{4,0},{5,1},{6,2},{7,3},{8,4},{9,5},{1... | collective-permute-start | bytes 1185800 | tf_op jit(solution)/shard_map/ppermute | solution.py:338
  59.1 0.0 collective-permute-done
  59.1 0.9 collective-permute-start.5
  60.0 1.8 %collective-permute-start.6 = (bf16[1544,128]{1,0:T(8,128)(2,1)}, bf16[1544,128]{1,0:T(8,128)(2,1)S(1)}, u32[]{:S(2)}, u32[]{:S(2)}) collective-permute-start(bf16[1544,128]{1,0:T(8,128)(2,1)} %get-tuple-element.43), channel_id=1, source_target_pairs={{0,14},{1,15},{2,0},{3,1},{4,2},{5,3},{6,4},{7,5},{8,6},{9,7},{10,... | collective-permute-start | bytes 1185800 | tf_op jit(solution)/shard_map/ppermute | solution.py:338
  61.8 0.0 collective-permute-done.2
  61.8 22.3 %conditional.2 = (bf16[8,584,128]{2,1,0:T(8,128)(2,1)S(1)}) conditional(s32[]{:T(128)} %bitcast.2, () %tuple.18, (bf16[1544,128]{1,0:T(8,128)(2,1)}, bf16[1544,128]{1,0:T(8,128)(2,1)}, bf16[1544,128]{1,0:T(8,128)(2,1)}) %tuple.19), branch_computations={%region_0.0_spmd, %region_1.0_spmd} | conditional | bytes 2392072 | solution.py:350
  61.8 1.4 %merge.1 = bf16[8,584,128]{2,1,0:T(8,128)(2,1)S(1)} custom-call(bf16[1544,128]{1,0:T(8,128)(2,1)} %get-tuple-element.15.refs_0_, bf16[1544,128]{1,0:T(8,128)(2,1)} %get-tuple-element.16.refs_1_, bf16[1544,128]{1,0:T(8,128)(2,1)} %get-tuple-element.17.refs_2_), custom_call_target="tpu_custom_call" | custom-call | tf_op jit(solution)/shard_map/cond/branch_1_fun/merge/pallas_call | solution.py:410
  63.2 21.0 %all_to_all.19 = bf16[8,584,128]{2,1,0:T(8,128)(2,1)S(1)} all-to-all(bf16[8,584,128]{2,1,0:T(8,128)(2,1)S(1)} %merge.1), channel_id=1, replica_groups={{0,1,16,17,32,33,48,49},{2,3,18,19,34,35,50,51},{4,5,20,21,36,37,52,53}..., dimensions={0} | all-to-all | bytes 2392064 | tf_op jit(solution)/shard_map/cond/branch_1_fun/all_to_all | solution.py:344
  84.1 0.0 collective-permute-done.3.refs_0_
  84.1 0.0 collective-permute-done.4.refs_1_
  84.1 3.4 %best_early.1.refs_5_ = f32[8,1536]{1,0:T(8,128)S(1)} custom-call(bf16[8,584,128]{2,1,0:T(8,128)(2,1)S(1)} %get-tuple-element.54.early_hbm, bf16[1544,128]{1,0:T(8,128)(2,1)S(1)} %collective-permute-done.3.refs_0_, bf16[1544,128]{1,0:T(8,128)(2,1)S(1)} %collective-permute-done.4.refs_1_, bf16[1544,128]{1,0:T(8,128)(2,1)S(1)} %copy-done), custom_call_target="tpu_custom_call" | custom-call | flops 1811939328 | bytes 8388608 | tf_op jit(solution)/shard_map/best_early/pallas_call | solution.py:424
  87.6 0.0 collective-permute-done.5.refs_3_
  87.6 3.2 %best_last.1 = f32[64,32]{1,0:T(8,128)S(1)} custom-call(bf16[8,584,128]{2,1,0:T(8,128)(2,1)S(1)} %get-tuple-element.54.early_hbm, bf16[1544,128]{1,0:T(8,128)(2,1)S(1)} %collective-permute-done.3.refs_0_, bf16[1544,128]{1,0:T(8,128)(2,1)S(1)} %collective-permute-done.4.refs_1_, bf16[1544,128]{1,0:T(8,128)(2,1)S(1)} %copy-done, ...), custom_call_target="tpu_custom_call" | custom-call | flops 3221225472 | bytes 8388608 | tf_op jit(solution)/shard_map/best_last/pallas_call | solution.py:424
  90.8 13.5 %all_to_all.21 = f32[64,1,32]{2,1,0:T(1,128)S(1)} all-to-all(f32[64,1,32]{2,1,0:T(1,128)S(1)} %bitcast.9), channel_id=1, replica_groups=mesh['outer'=4,'member'=64] {'member'}, dimensions={0} | all-to-all | bytes 16384 | tf_op jit(solution)/shard_map/all_to_all | solution.py:443
  104.4 1.0 home.1
  (4 shorter events, 0.0 us)
Async XLA Ops:
  3.2 55.9 %collective-permute-start = (bf16[1544,128]{1,0:T(8,128)(2,1)S(1)}, bf16[1544,128]{1,0:T(8,128)(2,1)}, u32[]{:S(2)}, u32[]{:S(2)}) collective-permute-start(bf16[1544,128]{1,0:T(8,128)(2,1)S(1)} %get-tuple-element.32), channel_id=1, source_target_pairs={{0,8},{1,9},{2,10},{3,11},{4,12},{5,13},{6,14},{7,15},{8,0},{9,1},... | collective-permute-start | bytes 1185800 | tf_op jit(solution)/shard_map/ppermute | solution.py:338
  17.5 42.5 %collective-permute-start.1 = (bf16[1544,128]{1,0:T(8,128)(2,1)S(1)}, bf16[1544,128]{1,0:T(8,128)(2,1)}, u32[]{:S(2)}, u32[]{:S(2)}) collective-permute-start(bf16[1544,128]{1,0:T(8,128)(2,1)S(1)} %get-tuple-element.36), channel_id=1, source_target_pairs={{0,6},{1,7},{2,8},{3,9},{4,10},{5,11},{6,12},{7,13},{8,14},{9,15},... | collective-permute-start | bytes 1185800 | tf_op jit(solution)/shard_map/ppermute | solution.py:338
  19.2 42.6 %collective-permute-start.2 = (bf16[1544,128]{1,0:T(8,128)(2,1)S(1)}, bf16[1544,128]{1,0:T(8,128)(2,1)}, u32[]{:S(2)}, u32[]{:S(2)}) collective-permute-start(bf16[1544,128]{1,0:T(8,128)(2,1)S(1)} %get-tuple-element.37), channel_id=1, source_target_pairs={{0,10},{1,11},{2,12},{3,13},{4,14},{5,15},{6,0},{7,1},{8,2},{9,3},... | collective-permute-start | bytes 1185800 | tf_op jit(solution)/shard_map/ppermute | solution.py:338
  55.5 28.6 %collective-permute-start.3 = (bf16[1544,128]{1,0:T(8,128)(2,1)}, bf16[1544,128]{1,0:T(8,128)(2,1)S(1)}, u32[]{:S(2)}, u32[]{:S(2)}) collective-permute-start(bf16[1544,128]{1,0:T(8,128)(2,1)} %get-tuple-element.39), channel_id=1, source_target_pairs={{0,4},{1,5},{2,6},{3,7},{4,8},{5,9},{6,10},{7,11},{8,12},{9,13},{1... | collective-permute-start | bytes 1185800 | tf_op jit(solution)/shard_map/ppermute | solution.py:338
  56.9 27.3 %collective-permute-start.4 = (bf16[1544,128]{1,0:T(8,128)(2,1)}, bf16[1544,128]{1,0:T(8,128)(2,1)S(1)}, u32[]{:S(2)}, u32[]{:S(2)}) collective-permute-start(bf16[1544,128]{1,0:T(8,128)(2,1)} %get-tuple-element.40), channel_id=1, source_target_pairs={{0,12},{1,13},{2,14},{3,15},{4,0},{5,1},{6,2},{7,3},{8,4},{9,5},{1... | collective-permute-start | bytes 1185800 | tf_op jit(solution)/shard_map/ppermute | solution.py:338
  59.1 28.5 %collective-permute-start.5 = (bf16[1544,128]{1,0:T(8,128)(2,1)}, bf16[1544,128]{1,0:T(8,128)(2,1)S(1)}, u32[]{:S(2)}, u32[]{:S(2)}) collective-permute-start(bf16[1544,128]{1,0:T(8,128)(2,1)} %get-tuple-element.42), channel_id=1, source_target_pairs={{0,2},{1,3},{2,4},{3,5},{4,6},{5,7},{6,8},{7,9},{8,10},{9,11},{10,... | collective-permute-start | bytes 1185800 | tf_op jit(solution)/shard_map/ppermute | solution.py:338
  60.0 27.6 %collective-permute-start.6 = (bf16[1544,128]{1,0:T(8,128)(2,1)}, bf16[1544,128]{1,0:T(8,128)(2,1)S(1)}, u32[]{:S(2)}, u32[]{:S(2)}) collective-permute-start(bf16[1544,128]{1,0:T(8,128)(2,1)} %get-tuple-element.43), channel_id=1, source_target_pairs={{0,14},{1,15},{2,0},{3,1},{4,2},{5,3},{6,4},{7,5},{8,6},{9,7},{10,... | collective-permute-start | bytes 1185800 | tf_op jit(solution)/shard_map/ppermute | solution.py:338
  61.8 22.3 %copy-start = (bf16[1544,128]{1,0:T(8,128)(2,1)S(1)}, bf16[1544,128]{1,0:T(8,128)(2,1)}, u32[]{:S(2)}) copy-start(bf16[1544,128]{1,0:T(8,128)(2,1)} %get-tuple-element.41.refs_2_) | copy-start | bytes 1185796
